TPU v7x, 512 devices: a whole 4x4x16 slice. The times are simulated.
512 devices in a mesh: dp: 2 (over x_lo), table: 32 (over z, core), tensor: 8 (over x_hi, y).
Axes of the slice: x: 4 (x_hi: 2, x_lo: 2; x = x_hi * 2 + x_lo), y: 4, z: 16, core: 2. Of those that a mesh axis runs over, the one named last changes fastest.
Arguments:
- fetched_table_entries: bfloat16 [64, 1024, 512], P('table', 'dp', 'tensor'), may hold values from -32 to 32
- position_category_number: int32 [64], replicated, may hold values from 0 to 63, each once
- category_shift_vector: float32 [64, 512], P(None, 'tensor'), may hold values from -6 to 6
- asker_matcher_content_matrix: bfloat16 [512, 3, 512], P(None, None, 'tensor'), may hold values from -0.25 to 0.25
- affinity_sharpness: float32 [8], P('tensor'), may hold values from 2 to 8
- mixer_exit_matrix: bfloat16 [512, 512], P('tensor'), may hold values from -0.25 to 0.25
- mixer_rescale_factor: float32 [512], replicated, may hold values from 0.5 to 1.5
- interact_matrix: bfloat16 [512, 512], P(None, 'tensor'), may hold values from -0.25 to 0.25
- interact_offset_vector: float32 [512], P('tensor'), may hold values from -4 to 4
- widening_matrix: bfloat16 [512, 4096], P(None, 'tensor'), may hold values from -0.25 to 0.25
- narrowing_matrix: bfloat16 [4096, 512], P('tensor'), may hold values from -0.09375 to 0.09375
- incoming_cotangent: bfloat16 [1024, 64, 512], P(('dp', 'table')), may hold values from -0.25 to 0.25
Outputs:
- mixed: bfloat16 [1024, 64, 512], P(('dp', 'table'), None, 'tensor')
- grad_cross: float32 [512, 512], P(None, 'tensor')
- grad_bias: float32 [512], P('tensor')
- grad_up: float32 [512, 4096], P(None, 'tensor')
- grad_down: float32 [4096, 512], P('tensor')
Inputs may be any that keep to these rules, and one draw needn't show every extreme that they name: `position_category_number`: slots are numbered in the order of the table axis, 64 // 32 to a device; each feature sits in exactly one slot.
All inputs are finite; a program needn't handle non-finite values.
Results may differ from a plain program's by a relative error of at most 0.023.
Values may be sent and summed in bfloat16 or wider, within the bound.
A program may use at most 64 MiB of HBM per device.

v0:
```python
import jax
import jax.numpy as jnp
from jax import lax
from jax.sharding import PartitionSpec as P

epsilon = 1e-06


def unit_rows(values):
    return values * lax.rsqrt(jnp.mean(values * values, axis=-1, keepdims=True) + epsilon)


def body(
    fetched_table_entries,
    position_category_number,
    category_shift_vector,
    asker_matcher_content_matrix,
    affinity_sharpness,
    mixer_exit_matrix,
    mixer_rescale_factor,
    interact_matrix,
    interact_offset_vector,
    widening_matrix,
    narrowing_matrix,
    incoming_cotangent,
):
    tensor_count = lax.axis_size("tensor")
    tensor_index = lax.axis_index("tensor")
    arrived = lax.all_to_all(
        fetched_table_entries, "table", split_axis=1, concat_axis=0, tiled=True
    )
    fields = position_category_number.shape[0]
    onehot = (
        position_category_number[None, :] == jnp.arange(fields, dtype=jnp.int32)[:, None]
    ).astype(jnp.bfloat16)
    placed = jnp.einsum("fs,sbd->bfd", onehot, arrived, preferred_element_type=jnp.float32)
    inputs = (placed + category_shift_vector[None]).astype(jnp.bfloat16)
    sample_count, _, width_local = inputs.shape
    row_count = sample_count * fields
    model_width = width_local * tensor_count
    input_rows = inputs.reshape(row_count, width_local)
    projection = asker_matcher_content_matrix.reshape(model_width, 3 * width_local)
    projected = jnp.dot(
        lax.all_gather(input_rows, "tensor", axis=1, tiled=True),
        projection,
        preferred_element_type=jnp.float32,
    )
    resident_group_total = affinity_sharpness.shape[0]
    per_group_span = width_local // resident_group_total
    shape_four = (sample_count, fields, resident_group_total, per_group_span)
    query_unit = unit_rows(projected[:, :width_local].reshape(shape_four)).astype(jnp.bfloat16)
    key_unit = unit_rows(projected[:, width_local : 2 * width_local].reshape(shape_four)).astype(
        jnp.bfloat16
    )
    value_rows = projected[:, 2 * width_local :].reshape(shape_four).astype(jnp.bfloat16)
    raw_affinity_logits = jnp.einsum(
        "bihe,bjhe->bhij", query_unit, key_unit, preferred_element_type=jnp.float32
    )
    affinity_matrix = (
        raw_affinity_logits * (affinity_sharpness / per_group_span)[None, :, None, None]
    )
    exponent = jnp.exp(affinity_matrix)
    attention = (exponent / jnp.sum(exponent, axis=-1, keepdims=True)).astype(jnp.bfloat16)
    heads = jnp.einsum("bhij,bjhe->bihe", attention, value_rows, preferred_element_type=jnp.float32)
    heads = heads.astype(jnp.bfloat16).reshape(row_count, width_local)
    own_columns = input_rows.astype(jnp.float32)
    partial_value = jnp.dot(heads, mixer_exit_matrix, preferred_element_type=jnp.float32)
    residual = lax.dynamic_update_slice_in_dim(
        jnp.zeros((row_count, model_width), jnp.float32), own_columns, tensor_index * width_local, 1
    )
    partial_value = partial_value + residual
    summed = lax.psum(partial_value.astype(jnp.bfloat16), "tensor").astype(jnp.float32)
    normed = (unit_rows(summed) * mixer_rescale_factor).astype(jnp.bfloat16)
    normed_local = lax.dynamic_slice_in_dim(normed, tensor_index * width_local, width_local, 1)
    crossed = own_columns * (
        jnp.dot(normed, interact_matrix, preferred_element_type=jnp.float32)
        + interact_offset_vector
    ) + normed_local.astype(jnp.float32)
    cotangent = incoming_cotangent.reshape(row_count, model_width)
    cotangent_local = lax.dynamic_slice_in_dim(
        cotangent, tensor_index * width_local, width_local, 1
    )
    cross_term = cotangent_local.astype(jnp.float32) * own_columns
    grad_bias = jnp.sum(cross_term, axis=0)
    grad_cross = jnp.dot(
        normed.T, cross_term.astype(jnp.bfloat16), preferred_element_type=jnp.float32
    )
    hidden_pre = jnp.dot(normed, widening_matrix, preferred_element_type=jnp.float32)
    activation = jax.nn.silu(hidden_pre).astype(jnp.bfloat16)
    grad_down = jnp.dot(activation.T, cotangent, preferred_element_type=jnp.float32)
    projected_down = lax.psum_scatter(
        jnp.dot(activation, narrowing_matrix, preferred_element_type=jnp.float32).astype(
            jnp.bfloat16
        ),
        "tensor",
        scatter_dimension=1,
        tiled=True,
    ).astype(jnp.float32)
    mixed = (
        (crossed + projected_down).astype(jnp.bfloat16).reshape(sample_count, fields, width_local)
    )
    back_act = jnp.dot(cotangent, narrowing_matrix.T, preferred_element_type=jnp.float32)
    sigma = jax.nn.sigmoid(hidden_pre)
    slope = (back_act * sigma * (1.0 + hidden_pre * (1.0 - sigma))).astype(jnp.bfloat16)
    grad_up = jnp.dot(normed.T, slope, preferred_element_type=jnp.float32)
    grad_cross, grad_bias, grad_up, grad_down = lax.psum(
        (grad_cross, grad_bias, grad_up, grad_down), ("dp", "table")
    )
    return (mixed, grad_cross, grad_bias, grad_up, grad_down)


def solution(mesh):
    in_specs = (
        P("table", "dp", "tensor"),
        P(),
        P(None, "tensor"),
        P(None, None, "tensor"),
        P("tensor"),
        P("tensor", None),
        P(),
        P(None, "tensor"),
        P("tensor"),
        P(None, "tensor"),
        P("tensor", None),
        P(("dp", "table"), None, None),
    )
    out_specs = (
        P(("dp", "table"), None, "tensor"),
        P(None, "tensor"),
        P("tensor"),
        P(None, "tensor"),
        P("tensor", None),
    )
    return jax.shard_map(body, mesh=mesh, in_specs=in_specs, out_specs=out_specs, check_vma=False)
```

profile of v0, /device:TPU:1, one launch (start us, length us, event | category | flops | bytes accessed | tf_op | source)
XLA Modules:
  0.0 740.7 jit_solution(5883140085415785041)
XLA Ops:
  7.2 0.0 all-gather.2.cloned.1.call-start
  7.2 1.1 copy.35
  8.4 0.2 reshape.133
  8.6 32.4 %all_to_all.18 = bf16[32,2,1024]{2,1,0:T(2,128)(2,1)S(1)} all-to-all(bf16[32,2,1024]{2,1,0:T(2,128)(2,1)S(1)} %reshape.133), channel_id=1, replica_groups=mesh['dp'=2,'table'=32,'tensor'=8] {'table'}, dimensions={0} | all-to-all | bytes 262144 | tf_op jit(solution)/shard_map/all_to_all | solution.py:29
  41.0 0.2 reshape.134
  41.3 0.3 copy.37
  41.6 0.2 fusion.4
  41.8 0.8 copy.38
  42.6 0.0 all-gather.2.cloned.1.call-update
  42.6 0.0 all-reduce.4.cloned.1.call-start
  43.3 0.1 constant_dynamic-slice_fusion
  43.5 0.1 copy.51
  43.6 51.6 %all-gather.2.cloned.1.call-done = bf16[1024,512]{0,1:T(8,128)(2,1)} async-done(((bf16[1024,64]{0,1:T(8,128)(2,1)}), bf16[1024,512]{0,1:T(8,128)(2,1)}) %all-gather.2.cloned.1.call-update) | async-done | bytes 1048592 | tf_op jit(solution)/shard_map/all_gather | solution.py:44
  95.2 1.6 fusion.29
  96.8 0.1 multiply_reduce_fusion.1
  96.9 0.1 rsqrt.33
  97.0 0.1 rsqrt.31
  97.0 0.2 convert_element_type.78
  97.2 0.2 copy.49
  97.4 0.2 copy.48
  97.6 0.7 fusion.3
  98.3 0.2 fusion.6
  98.6 0.2 copy.44
  98.8 0.2 reshape.129
  99.0 0.5 fusion.27
  99.5 0.0 copy-done.1
  99.5 0.2 fusion.18
  99.7 1.1 convert_element_type.85
  100.8 0.0 all-reduce.4.cloned.1.call-update
  100.8 0.0 reduce-scatter.2.cloned.1.call-start
  100.9 98.9 %all-reduce.4.cloned.1.call-done = bf16[1024,512]{0,1:T(8,128)(2,1)} async-done(((bf16[1024,512]{0,1:T(8,128)(2,1)}), bf16[1024,512]{0,1:T(8,128)(2,1)}) %all-reduce.4.cloned.1.call-update) | async-done | bytes 1048592 | tf_op jit(solution)/shard_map/psum | solution.py:72
  199.8 1.5 fusion
  201.2 1.5 fusion.2
  202.8 2.6 multiply_convert_fusion.1
  205.4 3.0 convolution_convert_fusion
  208.3 0.0 reduce-scatter.2.cloned.1.call-update
  208.4 0.0 all-reduce.6.cloned.1.call-start
  208.4 1.1 fusion.20
  209.5 3.0 fusion.28
  212.5 4.3 fusion.5
  216.7 0.0 all-reduce.6.cloned.1.call-update
  216.8 110.3 %psum.37 = f32[64]{0:T(128)} all-reduce(f32[64]{0:T(128)S(1)} %get-tuple-element.27), channel_id=1, replica_groups=mesh['dp'=2,'table'=32,'tensor'=8] {'dp','table'}, use_global_device_ids=true, to_apply=%region_8.9 | all-reduce | flops 64 | bytes 512 | tf_op jit(solution)/shard_map/psum | solution.py:106
  327.1 1.2 fusion.10
  328.3 0.8 copy.50
  329.2 400.1 %all-reduce.6.cloned.1.call-done = (f32[512,64]{0,1:T(8,128)}, f32[512,512]{1,0:T(8,128)}, f32[512,512]{1,0:T(8,128)}) async-done(((f32[512,64]{0,1:T(8,128)}, f32[512,512]{1,0:T(8,128)}, f32[512,512]{1,0:T(8,128)}), (f32[512,64]{0,1:T(8,128)}, f32[512,512]{1,0:T(8,128)}, f32[512,512]{1,0:T(8,128)})) %all-reduce.6.cloned.1.call-update) | async-done | bytes 2228240 | tf_op jit(solution)/shard_map/psum | solution.py:106
  729.3 1.7 copy.60
  731.0 2.3 copy.61
  733.2 1.0 copy.62
  (28 shorter events, 0.1 us)
Async XLA Ops:
  7.2 36.1 %copy-start = (bf16[16,64,512]{2,1,0:T(8,128)(2,1)S(1)}, bf16[16,64,512]{2,1,0:T(8,128)(2,1)}, u32[]{:S(2)}) copy-start(bf16[16,64,512]{2,1,0:T(8,128)(2,1)} %param.23) | copy-start | bytes 3145732
  7.2 34.4 %copy-start.6 = (f32[64,64]{1,0:T(8,128)S(1)}, f32[64,64]{1,0:T(8,128)}, u32[]{:S(2)}) copy-start(f32[64,64]{1,0:T(8,128)} %param.14) | copy-start | bytes 49156
  7.2 34.4 %copy-start.9 = (s32[64]{0:T(128)S(1)}, s32[64]{0:T(128)}, u32[]{:S(2)}) copy-start(s32[64]{0:T(128)} %param.13) | copy-start | bytes 772
  7.2 88.0 %all-gather.2.cloned.1.call-start = ((), (), s32[]{:S(2)}) async-start(), calls=%async_computation.2 | async-start | bytes 1179648 | tf_op jit(solution)/shard_map/all_gather | solution.py:44
  8.4 86.8 %copy-start.3 = (bf16[512,3,64]{0,2,1:T(8,128)(2,1)S(1)}, bf16[512,3,64]{0,2,1:T(8,128)(2,1)}, u32[]{:S(2)}) copy-start(bf16[512,3,64]{0,2,1:T(8,128)(2,1)} %param.15) | copy-start | bytes 589828
  42.6 157.2 %all-reduce.4.cloned.1.call-start = ((), (), s32[]{:S(2)}) async-start(), calls=%async_computation.3 | async-start | bytes 2097152 | tf_op jit(solution)/shard_map/psum | solution.py:72
  97.6 1.4 copy-start.4
  98.6 0.9 copy-start.1
  99.7 101.6 %copy-start.7 = (f32[512]{0:T(512)S(1)}, f32[512]{0:T(512)}, u32[]{:S(2)}) copy-start(f32[512]{0:T(512)} %param.18) | copy-start | bytes 6148
  100.8 101.9 %copy-start.10 = (bf16[512,512]{1,0:T(8,128)(2,1)S(1)}, bf16[512,512]{1,0:T(8,128)(2,1)}, u32[]{:S(2)}) copy-start(bf16[512,512]{1,0:T(8,128)(2,1)} %param.21) | copy-start | bytes 1572868
  100.8 226.3 %reduce-scatter.2.cloned.1.call-start = ((), (), s32[]{:S(2)}) async-start(), calls=%async_computation.4 | async-start | bytes 1179648 | tf_op jit(solution)/shard_map/reduce_scatter | solution.py:91
  202.8 2.6 copy-start.11
  208.4 520.9 %all-reduce.6.cloned.1.call-start = ((), (), s32[]{:S(2)}) async-start(), calls=%async_computation.5 | async-start | bytes 4456448 | tf_op jit(solution)/shard_map/psum | solution.py:106
  216.7 110.4 %copy-start.5 = (bf16[512,64]{0,1:T(8,128)(2,1)S(1)}, bf16[512,64]{0,1:T(8,128)(2,1)}, u32[]{:S(2)}) copy-start(bf16[512,64]{0,1:T(8,128)(2,1)} %param.19) | copy-start | bytes 196612
  216.7 110.4 %copy-start.8 = (f32[64]{0:T(128)S(1)}, f32[64]{0:T(128)}, u32[]{:S(2)}) copy-start(f32[64]{0:T(128)} %param.20) | copy-start | bytes 772
  729.3 3.9 copy-start.2
Sparse Core Ops, SparseCore 0:
  42.7 52.3 all-gather.1
  101.0 98.7 all-reduce.3
  208.5 87.9 reduce-scatter.1
  300.3 428.9 all-reduce.5
where the time goes:
time: 741 us
  waiting for transfers between devices  551 us (74%)
  blocking collectives  143 us (19%)
  matrix products  18.3 us (2%)
  between operations  14.7 us (2%)
  local copies, waits for them, and re-layouts  9.82 us (1%)
    psum x1, waiting for transfers between devices, body(): lax.psum((grad_cross, grad_bias, grad_up, grad_down), ('dp', 'table'))  400 us
    psum x1, blocking collectives, body(): lax.psum((grad_cross, grad_bias, grad_up, grad_down), ('dp', 'table'))  110 us
    psum x1, waiting for transfers between devices, body(): lax.psum(partial_value.astype(jnp.bfloat16), 'tensor').astype(jnp.float32)  98.9 us
    all_gather x1, waiting for transfers between devices, body(): lax.all_gather(input_rows, 'tensor', axis=1, tiled=True)  51.6 us
    all_to_all x1, blocking collectives, body(): lax.all_to_all(fetched_table_entries, 'table', split_axis=1, concat_axis=...  32.4 us
  transfers between devices with their start and end apart: 4, of which 3 were waited for; matrix products, arithmetic and copies ran while one was open for 1% of the time, Pallas kernels for 0%

commit v1 on v0

v1 whole, which is shorter than its diff:
```python
import functools

import jax
import jax.numpy as jnp
from jax import lax
from jax.experimental import pallas as pl
from jax.experimental.pallas import tpu as pltpu
from jax.sharding import PartitionSpec as P

MESH = pl.DeviceIdType.MESH
F32, BF16 = jnp.float32, jnp.bfloat16
EPS = 1e-06

TABLE, TENSOR, Z = 32, 8, 16
CHUNK = 144
CLASS = 4 * CHUNK
HALF = 4 * CLASS
ROWS = 2 * HALF


def nn(a, b):
    return jnp.dot(a, b, preferred_element_type=F32)


def nt(a, b):
    return lax.dot_general(a, b, (((1,), (1,)), ((), ())), preferred_element_type=F32)


def iota(shape, dim):
    return lax.broadcasted_iota(jnp.int32, shape, dim)


def remote(src, dst, send, recv, **device):
    return pltpu.make_async_remote_copy(
        src_ref=src, dst_ref=dst, send_sem=send, recv_sem=recv, device_id=device, device_id_type=MESH
    )


def kernel(
    f_ref, pos_ref, shift_ref, wqkv_ref, sharp_ref, mex_ref, gain_ref, int_ref, off_ref, wup_ref, wdn_ref, cot_ref,
    mixed_ref, gu_ref, gd_ref, gc_ref, gb_ref,
    zs, arr, arrf, xin, xa, own4, all4, own_sharp, all_sharp, xrow, nall, back, wup_t, wdn_t, low, xt, ctt, mlp, rs, cross,
    g32, gb16, crecv, h32, hb16, nr, c32, cb16, fr, fb16, dr, gfin,
    zss, zrs, tss, trs, wss, wrs, css, crs, sss, srs, ass, ars, mss, mrs, gss, grs,
):
    dp = lax.axis_index("dp")
    table = lax.axis_index("table")
    tensor = lax.axis_index("tensor")
    z, core = table // 2, lax.rem(table, 2)
    hi, y = tensor // 4, lax.rem(tensor, 4)
    sibling = table + 1 - 2 * core

    def around(k):
        return lax.rem(table + TABLE + k, TABLE)

    def tensor_at(k):
        return lax.rem(tensor + k, TENSOR)

    barrier = pltpu.get_barrier_semaphore()
    for k in range(1, TABLE):
        pl.semaphore_signal(barrier, inc=1, device_id={"table": around(k)}, device_id_type=MESH)
    for k in range(1, TENSOR):
        pl.semaphore_signal(barrier, inc=1, device_id={"tensor": tensor_at(k)}, device_id_type=MESH)
    pl.semaphore_signal(barrier, inc=1, device_id={"dp": 1 - dp}, device_id_type=MESH)

    zs[...] = f_ref[...].T
    arr[TABLE - 1] = zs[pl.ds(pl.multiple_of(16 * table, 16), 16), :]
    own4[0:3] = wqkv_ref[...]
    own4[3] = mex_ref[...]
    own_sharp[...] = jnp.broadcast_to(sharp_ref[...], own_sharp.shape)
    wup_t[...] = wup_ref[...].T
    wdn_t[...] = wdn_ref[...].T
    low[0:64] = int_ref[...]
    low[64:128] = (iota((64, 512), 1) == 64 * tensor + iota((64, 512), 0)).astype(F32).astype(BF16)
    def backward(i, carry):
        rows = cot_ref[pl.ds(pl.multiple_of(128 * i, 128), 128), :]
        back[i] = nt(wdn_ref[...], rows)
        ctt[i] = nt(low[64:128], rows)
        return carry
    lax.fori_loop(0, TENSOR, backward, 0)
    g32[...] = jnp.zeros_like(g32)

    lane = iota((1, 128), 1)
    left = lane < 64
    hot = (iota((64, 64), 0) == pos_ref[...]).astype(F32).astype(BF16)
    j = iota((64, 64), 1)
    source = 2 * lax.rem(table - lax.rem(j, 32) - 1 + TABLE, TABLE) + j // 32
    place = nn(hot, (iota((64, 64), 0) == source).astype(F32).astype(BF16)).astype(BF16)
    shift = shift_ref[...]
    shift = jnp.concatenate([shift, shift], axis=1)

    pl.semaphore_wait(barrier, TABLE - 1 + TENSOR - 1 + 1)

    to_table = []
    for d in (8, 7, 9, 6, 10, 5, 11, 4, 12, 3, 13, 2, 14, 1, 15, 0):
        for k in (2 * d, 2 * d + 1):
            if k == 0:
                continue
            rows = zs.at[pl.ds(pl.multiple_of(16 * around(k), 16), 16), :]
            copy = remote(rows, arr.at[k - 1], zss.at[k], zrs.at[k], table=around(k))
            copy.start()
            to_table.append(copy)

    pair = pl.ds(2 * core, 2)
    mine = pl.ds(pl.multiple_of(64 * tensor, 64), 64)
    all4[pair, mine, :] = own4[pair]
    all_sharp[tensor] = own_sharp[...]
    weights, sharps = [], []
    for k in range(1, TENSOR):
        copy = remote(own_sharp, all_sharp.at[tensor], sss.at[k], srs.at[k], tensor=tensor_at(k))
        copy.start()
        sharps.append(copy)
    for k in range(1, TENSOR):
        copy = remote(own4.at[pair], all4.at[pair, mine, :], wss.at[k], wrs.at[k], tensor=tensor_at(k))
        copy.start()
        weights.append(copy)

    for copy in to_table:
        copy.wait_recv()
    arrf[...] = arr[...].astype(F32)
    for i in range(TENSOR):
        a, b = arrf[:, 2 * i, :], arrf[:, 2 * i + 1, :]
        even = jnp.where(left, a, pltpu.roll(b, 64, 1))
        odd = jnp.where(left, pltpu.roll(a, 64, 1), b)
        rows = jnp.concatenate([even, odd], axis=0).astype(BF16)
        xin[i] = (nn(place, rows) + shift).astype(BF16)
    to_tensor = []
    for k in range(1, TENSOR):
        copy = remote(xin.at[tensor_at(k)], xa.at[tensor], tss.at[k], trs.at[k], tensor=tensor_at(k))
        copy.start()
        to_tensor.append(copy)
    xa[tensor] = xin[tensor]

    def columns(i, carry):
        t = xin[i].astype(F32).T
        xt[i] = jnp.concatenate([t[0:64], t[64:128]], axis=1)
        return carry
    lax.fori_loop(0, TENSOR, columns, 0)
    term = ctt[...] * xt[...]
    ctt[...] = term
    bias = jnp.sum(jnp.sum(term, axis=0), axis=1, keepdims=True)

    for copy in weights:
        copy.wait_recv()
    over = remote(all4.at[pair], all4.at[pair], css.at[0], crs.at[0], table=sibling)
    over.start()
    for copy in to_tensor + sharps:
        copy.wait_recv()

    for i in range(4):
        a, b = xa[2 * i].astype(F32), xa[2 * i + 1].astype(F32)
        span = slice(128 * i, 128 * i + 128)
        xrow[0:64, span] = jnp.where(left, a, pltpu.roll(b, 64, 1)).astype(BF16)
        xrow[64:128, span] = jnp.where(left, pltpu.roll(a, 64, 1), b).astype(BF16)
    over.wait_recv()

    x = xrow[...]
    same_head = (iota((512, 512), 0) // 64 == iota((512, 512), 1) // 64).astype(F32).astype(BF16)

    def unit(v):
        squares = nn((v * v).astype(BF16), same_head)
        return v * lax.rsqrt(squares * (1.0 / 64) + EPS)

    query = unit(nt(x, all4[0]))
    key = unit(nt(x, all4[1])).astype(BF16)
    value = nt(x, all4[2])
    same_sample = iota((128, 128), 0) // 64 == iota((128, 128), 1) // 64
    heads = []
    for i in range(4):
        span = slice(128 * i, 128 * i + 128)
        q, k, v = query[:, span], key[:, span], value[:, span]
        parts = []
        for s in range(2):
            half = left if s == 0 else jnp.logical_not(left)
            scores = nt(jnp.where(half, q, 0.0).astype(BF16), k) * (all_sharp[2 * i + s, 0:1, :] * (1.0 / 64))
            e = jnp.where(same_sample, jnp.exp(scores), 0.0).astype(BF16)
            o = nn(e, jnp.where(half, v, 1.0).astype(BF16))
            parts.append(o / pltpu.roll(o, 64, 1))
        heads.append(jnp.where(left, parts[0], parts[1]).astype(BF16))
    summed = nn(jnp.concatenate(heads, axis=1), all4[3]) + x.astype(F32)
    mean = jnp.mean(summed * summed, axis=1, keepdims=True)
    nall[tensor] = (summed * lax.rsqrt(mean + EPS) * gain_ref[...]).astype(BF16)

    def relative(r, sign):
        dh, d = r // 4, lax.rem(r, 4)
        dy = d + (d // 2) * (5 - 2 * d)
        return 4 * lax.rem(hi + dh, 2) + lax.rem(y + 4 + sign * dy, 4)

    gathers = []
    for r in range(1, TENSOR):
        copy = remote(nall.at[tensor], nall.at[tensor], ass.at[r], ars.at[r], tensor=relative(r, 1))
        copy.start()
        gathers.append(copy)

    off = jnp.sum(jnp.where(iota((64, 64), 0) == iota((64, 64), 1), off_ref[...], 0.0), axis=1, keepdims=True)

    def chunk(r, carry):
        i = relative(r, -1)

        @pl.when(r > 0)
        def _():
            remote(nall.at[i], nall.at[i], ass.at[r], ars.at[r], tensor=i).wait_recv()

        n = nall[i]
        h = nt(wup_t[...], n)
        sg = 1.0 / (1.0 + jnp.exp(-h))
        act = (h * sg).astype(BF16)
        slope = (back[i] * sg * (1.0 + h * (1.0 - sg))).astype(BF16)
        mlp[i] = nn(wdn_t[...], act).astype(BF16)
        rows = cot_ref[pl.ds(pl.multiple_of(128 * i, 128), 128), :]
        down = nn(act, rows)
        up = nt(n.T, slope)
        side = nn(ctt[i].astype(BF16), n)
        for t in range(4):
            span = slice(128 * t, 128 * t + 128)
            g32[512 * t : 512 * t + 512] += up[:, span]
            g32[2048 + 512 * t : 2560 + 512 * t] += down[:, span]
            g32[4096 + 64 * t : 4160 + 64 * t] += side[:, span]
        c = nt(low[...], n)
        cross[i] = xt[i] * (c[0:64] + off) + c[64:128]
        return carry

    lax.fori_loop(0, TENSOR, chunk, 0)
    g32[4352:4416] = jnp.broadcast_to(bias, (64, 128))

    gb16[...] = g32[...].astype(BF16)
    mine_half = pl.ds(pl.multiple_of(HALF * core, 16), HALF)
    other_half = pl.ds(pl.multiple_of(HALF * (1 - core), 16), HALF)
    cores = remote(gb16.at[other_half], crecv, gss.at[0], grs.at[0], table=sibling)
    cores.start()
    terms = []
    for k in range(1, TENSOR):
        to = tensor_at(k)
        rows = mlp.at[:, pl.ds(pl.multiple_of(64 * to, 64), 64), :]
        copy = remote(rows, rs.at[k - 1], mss.at[k], mrs.at[k], tensor=to)
        copy.start()
        terms.append(copy)
    cores.wait_recv()
    h32[...] = g32[mine_half, :] + crecv[...].astype(F32)
    hb16[...] = h32[...].astype(BF16)

    def class_rows(q):
        return pl.ds(pl.multiple_of(CLASS * lax.rem(q, 4), 16), CLASS)

    near_by = (2, -2, 8 * core - 4)
    near_z = (1, -1, 4 * core - 2)
    near = []
    for i in range(3):
        copy = remote(
            hb16.at[class_rows(z + Z + near_z[i]), :], nr.at[i], gss.at[1 + i], grs.at[1 + i], table=around(near_by[i])
        )
        copy.start()
        near.append(copy)
    for copy in near:
        copy.wait_recv()
    c32[...] = h32[class_rows(z), :] + nr[0].astype(F32) + nr[1].astype(F32) + nr[2].astype(F32)
    cb16[...] = c32[...].astype(BF16)

    def chunk_rows(q):
        return pl.ds(pl.multiple_of(CHUNK * lax.rem(q // 4, 4), 16), CHUNK)

    far = []
    for i, k in enumerate((8, 4, 12)):
        copy = remote(cb16.at[chunk_rows(z + k), :], fr.at[i], gss.at[4 + i], grs.at[4 + i], table=around(2 * k))
        copy.start()
        far.append(copy)
    for copy in terms:
        copy.wait_recv()

    def finish(i, carry):
        own = mlp[i, pl.ds(pl.multiple_of(64 * tensor, 64), 64), :].astype(F32)
        for k in range(1, TENSOR):
            own = own + rs[k - 1, i].astype(F32)
        out = (cross[i] + own).T
        mixed_ref[2 * i] = out[0:64].astype(BF16)
        mixed_ref[2 * i + 1] = out[64:128].astype(BF16)
        return carry

    lax.fori_loop(0, TENSOR, finish, 0)
    for copy in far:
        copy.wait_recv()
    total = c32[chunk_rows(z), :] + fr[0].astype(F32) + fr[1].astype(F32) + fr[2].astype(F32)
    fb16[...] = total.astype(BF16)
    twin = remote(fb16, dr, gss.at[7], grs.at[7], dp=1 - dp)
    twin.start()
    twin.wait_recv()

    base = HALF * core + CLASS * lax.rem(z, 4)
    own_chunk = gfin.at[pl.ds(pl.multiple_of(base + CHUNK * (z // 4), 16), CHUNK), :]
    own_chunk[...] = (fb16[...].astype(F32) + dr[...].astype(F32)).astype(BF16)
    back_far = []
    for i, k in enumerate((8, 4, 12)):
        copy = remote(own_chunk, own_chunk, gss.at[8 + i], grs.at[8 + i], table=around(2 * k))
        copy.start()
        back_far.append(copy)
    for copy in back_far:
        copy.wait_recv()
    own_class = gfin.at[pl.ds(pl.multiple_of(base, 16), CLASS), :]
    back_near = []
    for i in range(3):
        copy = remote(own_class, own_class, gss.at[11 + i], grs.at[11 + i], table=around(near_by[i]))
        copy.start()
        back_near.append(copy)
    across = [remote(own_class, own_class, gss.at[14], grs.at[14], table=sibling)]
    across[0].start()
    for i in range(3):
        back_near[i].wait_recv()
        q = z + Z - near_z[i]
        block = gfin.at[pl.ds(pl.multiple_of(HALF * core + CLASS * lax.rem(q, 4), 16), CLASS), :]
        copy = remote(block, block, gss.at[15 + i], grs.at[15 + i], table=sibling)
        copy.start()
        across.append(copy)
    for copy in across:
        copy.wait_recv()

    for t in range(4):
        span = slice(128 * t, 128 * t + 128)
        gu_ref[:, span] = gfin[512 * t : 512 * t + 512]
        gd_ref[:, span] = gfin[2048 + 512 * t : 2560 + 512 * t]
        gc_ref[:, span] = gfin[4096 + 64 * t : 4160 + 64 * t]
    gb_ref[...] = gfin[4352:4416]

    every = to_table + to_tensor + weights + sharps + [over] + gathers + [cores] + terms + near + far
    for copy in every + [twin] + back_far + back_near + across:
        copy.wait_send()


def body(
    fetched_table_entries,
    position_category_number,
    category_shift_vector,
    asker_matcher_content_matrix,
    affinity_sharpness,
    mixer_exit_matrix,
    mixer_rescale_factor,
    interact_matrix,
    interact_offset_vector,
    widening_matrix,
    narrowing_matrix,
    incoming_cotangent,
):
    vmem = pl.BlockSpec(memory_space=pltpu.VMEM)
    operands = (
        jnp.transpose(fetched_table_entries, (0, 2, 1)).reshape(128, 512),
        position_category_number.reshape(1, 64),
        category_shift_vector,
        jnp.transpose(asker_matcher_content_matrix, (1, 2, 0)),
        affinity_sharpness.reshape(1, 1),
        mixer_exit_matrix,
        mixer_rescale_factor.reshape(1, 512),
        interact_matrix.T,
        interact_offset_vector.reshape(1, 64),
        widening_matrix,
        narrowing_matrix,
        incoming_cotangent.reshape(1024, 512),
    )
    dma = pltpu.SemaphoreType.DMA
    scratch = [
        pltpu.VMEM((512, 128), BF16),
        pltpu.VMEM((32, 16, 128), BF16),
        pltpu.VMEM((32, 16, 128), F32),
        pltpu.VMEM((8, 64, 128), BF16),
        pltpu.VMEM((8, 64, 128), BF16),
        pltpu.VMEM((4, 64, 512), BF16),
        pltpu.VMEM((4, 512, 512), BF16),
        pltpu.VMEM((8, 128), F32),
        pltpu.VMEM((8, 8, 128), F32),
        pltpu.VMEM((128, 512), BF16),
        pltpu.VMEM((8, 128, 512), BF16),
        pltpu.VMEM((8, 512, 128), F32),
        pltpu.VMEM((512, 512), BF16),
        pltpu.VMEM((512, 512), BF16),
        pltpu.VMEM((128, 512), BF16),
        pltpu.VMEM((8, 64, 128), F32),
        pltpu.VMEM((8, 64, 128), F32),
        pltpu.VMEM((8, 512, 128), BF16),
        pltpu.VMEM((7, 8, 64, 128), BF16),
        pltpu.VMEM((8, 64, 128), F32),
        pltpu.VMEM((ROWS, 128), F32),
        pltpu.VMEM((ROWS, 128), BF16),
        pltpu.VMEM((HALF, 128), BF16),
        pltpu.VMEM((HALF, 128), F32),
        pltpu.VMEM((HALF, 128), BF16),
        pltpu.VMEM((3, CLASS, 128), BF16),
        pltpu.VMEM((CLASS, 128), F32),
        pltpu.VMEM((CLASS, 128), BF16),
        pltpu.VMEM((3, CHUNK, 128), BF16),
        pltpu.VMEM((CHUNK, 128), BF16),
        pltpu.VMEM((CHUNK, 128), BF16),
        pltpu.VMEM((ROWS, 128), BF16),
    ]
    for n in (32, 8, 8, 1, 8, 8, 8, 18):
        scratch += [dma((n,)), dma((n,))]
    mixed, up, down, cross, bias = pl.pallas_call(
        kernel,
        name="layer",
        out_shape=(
            jax.ShapeDtypeStruct((16, 64, 64), BF16),
            jax.ShapeDtypeStruct((512, 512), BF16),
            jax.ShapeDtypeStruct((512, 512), BF16),
            jax.ShapeDtypeStruct((64, 512), BF16),
            jax.ShapeDtypeStruct((64, 128), BF16),
        ),
        in_specs=[vmem] * len(operands),
        out_specs=(vmem,) * 5,
        scratch_shapes=scratch,
        compiler_params=pltpu.CompilerParams(
            collective_id=0, has_side_effects=True, vmem_limit_bytes=48 * 2**20
        ),
    )(*operands)
    return mixed, cross.astype(F32).T, bias[:, 0].astype(F32), up.astype(F32), down.astype(F32)


def solution(mesh):
    in_specs = (
        P("table", "dp", "tensor"),
        P(),
        P(None, "tensor"),
        P(None, None, "tensor"),
        P("tensor"),
        P("tensor", None),
        P(),
        P(None, "tensor"),
        P("tensor"),
        P(None, "tensor"),
        P("tensor", None),
        P(("dp", "table"), None, None),
    )
    out_specs = (
        P(("dp", "table"), None, "tensor"),
        P(None, "tensor"),
        P("tensor"),
        P(None, "tensor"),
        P("tensor", None),
    )
    return jax.shard_map(body, mesh=mesh, in_specs=in_specs, out_specs=out_specs, check_vma=False)
```

time: 741 us -> 116 us (0.16)
  waiting for transfers between devices: 551 us -> 0 us
  blocking collectives: 143 us -> 0 us
  Pallas kernels: 0 us -> 102 us
  matrix products: 18.3 us -> 0 us
  between operations: 14.7 us -> 1.33 us
    psum x2 -> x0, waiting for transfers between devices: 499 us -> none  [the longest x1 400 us: body(): lax.psum((grad_cross, grad_bias, grad_up, grad_down), ('dp', 'table'))]
    psum x1 -> x0, blocking collectives: 110 us -> none  [body(): lax.psum((grad_cross, grad_bias, grad_up, grad_down), ('dp', 'table'))]
    pallas_call x0 -> x1, Pallas kernels: none -> 102 us  [body(): pl.pallas_call(kernel, name='layer', out_shape=(jax.ShapeDtypeStruct((16,...]
    all_gather x1 -> x0, waiting for transfers between devices: 51.6 us -> none  [body(): lax.all_gather(input_rows, 'tensor', axis=1, tiled=True)]
    all_to_all x1 -> x0, blocking collectives: 32.4 us -> none  [body(): lax.all_to_all(fetched_table_entries, 'table', split_axis=1, concat_axis=...]
    dot_general x11 -> x0, matrix products: 18.3 us -> none  [the longest x1 4.26 us: body(): grad_up = jnp.dot(normed.T, slope, preferred_element_type=jnp.float32)]
  transfers between devices with their start and end apart: 4 -> 0, of which waited for: 3 -> 0; matrix products, arithmetic and copies ran while one was open for 1% -> 0% of each run, Pallas kernels for 0% -> 0%
where the time goes in v1:
time: 116 us
  Pallas kernels  102 us (88%)
  local copies, waits for them, and re-layouts  8.94 us (8%)
  other arithmetic  3.49 us (3%)
  between operations  1.33 us (1%)
    pallas_call x1, Pallas kernels, body(): pl.pallas_call(kernel, name='layer', out_shape=(jax.ShapeDtypeStruct((16,...  102 us
    unnamed x23, local copies, waits for them, and re-layouts  8.94 us

profile of v1, /device:TPU:1, one launch (start us, length us, event | category | flops | bytes accessed | tf_op | source)
XLA Modules:
  0.0 115.5 jit_solution(13744108916432005496)
XLA Ops:
  1.3 0.0 copy-start.8
  1.3 0.0 copy-start.9
  1.3 0.0 copy-start.10
  1.3 0.7 copy-done.8
  2.0 0.0 copy-done.9
  2.0 0.0 copy-done.10
  2.0 0.0 copy-start
  2.0 1.2 %copy-done = bf16[16,64,512]{2,1,0:T(8,128)(2,1)S(1)} copy-done((bf16[16,64,512]{2,1,0:T(8,128)(2,1)S(1)}, bf16[16,64,512]{2,1,0:T(8,128)(2,1)}, u32[]{:S(2)}) %copy-start) | copy-done | bytes 1048600
  3.2 0.0 copy-start.1
  3.2 1.0 copy-done.1
  4.2 0.0 copy-start.2
  4.2 1.0 copy-done.2
  5.3 0.0 copy-start.3
  5.3 0.9 copy-done.3
  6.2 0.0 copy-start.4
  6.2 0.9 copy-done.4
  7.1 0.0 copy-start.5
  7.1 0.8 copy-done.5
  8.0 0.0 copy-start.6
  8.0 0.8 copy-done.6
  8.8 0.0 copy-start.7
  8.8 0.8 copy-done.7
  9.6 101.8 %layer.1 = (bf16[16,64,64]{2,1,0:T(8,128)(2,1)S(1)}, bf16[512,512]{1,0:T(8,128)(2,1)S(1)}, bf16[512,512]{1,0:T(8,128)(2,1)S(1)}, bf16[64,512]{1,0:T(8,128)(2,1)S(1)}, bf16[64,128]{1,0:T(8,128)(2,1)S(1)}) custom-call(bf16[128,512]{1,0:T(8,128)(2,1)S(1)} %bitcast.15, s32[1,64]{1,0:T(1,128)S(1)} %bitcast.18, f32[64,64]{1,0:T(8,128)S(1)} %copy-done.7, ...), custom_call_target="tpu_custom_call" | custom-call | tf_op jit(solution)/shard_map/layer/pallas_call | solution.py:394
  111.3 1.1 convert_element_type.15
  112.4 1.1 convert_element_type.16
  113.5 0.7 convert_bitcast_fusion
  114.2 0.6 convert_reduce_fusion
  114.8 0.7 copy.19
Async XLA Ops:
  1.3 0.7 copy-start.8
  1.3 0.7 copy-start.9
  1.3 0.7 copy-start.10
  2.0 1.2 %copy-start = (bf16[16,64,512]{2,1,0:T(8,128)(2,1)S(1)}, bf16[16,64,512]{2,1,0:T(8,128)(2,1)}, u32[]{:S(2)}) copy-start(bf16[16,64,512]{2,1,0:T(8,128)(2,1)} %param.23) | copy-start | bytes 3145732
  3.2 1.0 copy-start.1
  4.2 1.0 copy-start.2
  5.3 0.9 copy-start.3
  6.2 0.9 copy-start.4
  7.1 0.8 copy-start.5
  8.0 0.8 copy-start.6
  8.8 0.8 copy-start.7

commit v2 on v1

--- a/solution.py
+++ b/solution.py
@@ -37,12 +37,22 @@
 
 
 def kernel(
-    f_ref, pos_ref, shift_ref, wqkv_ref, sharp_ref, mex_ref, gain_ref, int_ref, off_ref, wup_ref, wdn_ref, cot_ref,
-    mixed_ref, gu_ref, gd_ref, gc_ref, gb_ref,
+    f_hbm, pos_hbm, shift_hbm, wqkv_hbm, sharp_hbm, mex_hbm, gain_hbm, int_hbm, off_hbm, wup_hbm, wdn_hbm, cot_hbm,
+    mixed_ref, gfin,
+    f_ref, pos_ref, shift_ref, gain_ref, off_ref, sharp_ref, wup_ref, wdn_ref, cot_ref,
     zs, arr, arrf, xin, xa, own4, all4, own_sharp, all_sharp, xrow, nall, back, wup_t, wdn_t, low, xt, ctt, mlp, rs, cross,
-    g32, gb16, crecv, h32, hb16, nr, c32, cb16, fr, fb16, dr, gfin,
-    zss, zrs, tss, trs, wss, wrs, css, crs, sss, srs, ass, ars, mss, mrs, gss, grs,
+    g32, gb16, crecv, hb16, nr, c32, cb16, fr, fb16, dr,
+    zss, zrs, tss, trs, wss, wrs, css, crs, sss, srs, ass, ars, mss, mrs, gss, grs, los,
 ):
+    loads = []
+    for hbm, ref in (
+        (f_hbm, f_ref), (wup_hbm, wup_ref), (wdn_hbm, wdn_ref), (int_hbm, low.at[0:64]), (cot_hbm, cot_ref),
+        (wqkv_hbm, own4.at[0:3]), (mex_hbm, own4.at[3]), (pos_hbm, pos_ref), (shift_hbm, shift_ref),
+        (gain_hbm, gain_ref), (off_hbm, off_ref), (sharp_hbm, sharp_ref),
+    ):
+        copy = pltpu.make_async_copy(hbm, ref, los.at[len(loads)])
+        copy.start()
+        loads.append(copy)
     dp = lax.axis_index("dp")
     table = lax.axis_index("table")
     tensor = lax.axis_index("tensor")
@@ -63,14 +73,16 @@
         pl.semaphore_signal(barrier, inc=1, device_id={"tensor": tensor_at(k)}, device_id_type=MESH)
     pl.semaphore_signal(barrier, inc=1, device_id={"dp": 1 - dp}, device_id_type=MESH)
 
+    loads[0].wait()
     zs[...] = f_ref[...].T
     arr[TABLE - 1] = zs[pl.ds(pl.multiple_of(16 * table, 16), 16), :]
-    own4[0:3] = wqkv_ref[...]
-    own4[3] = mex_ref[...]
+    loads[1].wait()
+    wup_t[...] = wup_ref[...].T
+    loads[2].wait()
+    wdn_t[...] = wdn_ref[...].T
+    for copy in loads[3:]:
+        copy.wait()
     own_sharp[...] = jnp.broadcast_to(sharp_ref[...], own_sharp.shape)
-    wup_t[...] = wup_ref[...].T
-    wdn_t[...] = wdn_ref[...].T
-    low[0:64] = int_ref[...]
     low[64:128] = (iota((64, 512), 1) == 64 * tensor + iota((64, 512), 0)).astype(F32).astype(BF16)
     def backward(i, carry):
         rows = cot_ref[pl.ds(pl.multiple_of(128 * i, 128), 128), :]
@@ -224,10 +236,24 @@
     g32[4352:4416] = jnp.broadcast_to(bias, (64, 128))
 
     gb16[...] = g32[...].astype(BF16)
-    mine_half = pl.ds(pl.multiple_of(HALF * core, 16), HALF)
-    other_half = pl.ds(pl.multiple_of(HALF * (1 - core), 16), HALF)
-    cores = remote(gb16.at[other_half], crecv, gss.at[0], grs.at[0], table=sibling)
-    cores.start()
+
+    def owned(zz):
+        zz = lax.rem(zz + 2 * Z, Z)
+        return pl.multiple_of(CLASS * lax.rem(zz, 4) + CHUNK * (zz // 4), 16)
+
+    def rows_of(c, zz):
+        return pl.ds(pl.multiple_of(HALF * c + owned(zz), 16), CHUNK)
+
+    steps = (8, 4, 12, 0)
+    cores = []
+    for k in steps:
+        for d in (1, -1, 2 - 4 * core, 0):
+            n = len(cores)
+            copy = remote(
+                gb16.at[rows_of(1 - core, z + d + k), :], crecv.at[n], css.at[1 + n], crs.at[1 + n], table=sibling
+            )
+            copy.start()
+            cores.append(copy)
     terms = []
     for k in range(1, TENSOR):
         to = tensor_at(k)
@@ -235,35 +261,60 @@
         copy = remote(rows, rs.at[k - 1], mss.at[k], mrs.at[k], tensor=to)
         copy.start()
         terms.append(copy)
-    cores.wait_recv()
-    h32[...] = g32[mine_half, :] + crecv[...].astype(F32)
-    hb16[...] = h32[...].astype(BF16)
-
-    def class_rows(q):
-        return pl.ds(pl.multiple_of(CLASS * lax.rem(q, 4), 16), CLASS)
-
+
+    near_z = (1, -1, 4 * core - 2)
     near_by = (2, -2, 8 * core - 4)
-    near_z = (1, -1, 4 * core - 2)
     near = []
-    for i in range(3):
-        copy = remote(
-            hb16.at[class_rows(z + Z + near_z[i]), :], nr.at[i], gss.at[1 + i], grs.at[1 + i], table=around(near_by[i])
-        )
-        copy.start()
-        near.append(copy)
-    for copy in near:
+    for s, k in enumerate(steps):
+        for i in range(3):
+            n = 4 * s + i
+            cores[n].wait_recv()
+            part = g32[rows_of(core, z + near_z[i] + k), :] + crecv[n].astype(F32)
+            hb16[3 * s + i] = part.astype(BF16)
+            copy = remote(hb16.at[3 * s + i], nr.at[3 * s + i], gss.at[3 * s + i], grs.at[3 * s + i], table=around(near_by[i]))
+            copy.start()
+            near.append(copy)
+    far = []
+    for s, k in enumerate(steps):
+        n = 4 * s + 3
+        cores[n].wait_recv()
+        total = g32[rows_of(core, z + k), :] + crecv[n].astype(F32)
+        for i in range(3):
+            near[3 * s + i].wait_recv()
+            total = total + nr[3 * s + i].astype(F32)
+        if k:
+            cb16[s] = total.astype(BF16)
+            copy = remote(cb16.at[s], fr.at[s], gss.at[12 + s], grs.at[12 + s], table=around(2 * k))
+            copy.start()
+            far.append(copy)
+        else:
+            c32[...] = total
+    for copy in far:
         copy.wait_recv()
-    c32[...] = h32[class_rows(z), :] + nr[0].astype(F32) + nr[1].astype(F32) + nr[2].astype(F32)
-    cb16[...] = c32[...].astype(BF16)
-
-    def chunk_rows(q):
-        return pl.ds(pl.multiple_of(CHUNK * lax.rem(q // 4, 4), 16), CHUNK)
-
-    far = []
-    for i, k in enumerate((8, 4, 12)):
-        copy = remote(cb16.at[chunk_rows(z + k), :], fr.at[i], gss.at[4 + i], grs.at[4 + i], table=around(2 * k))
-        copy.start()
-        far.append(copy)
+    total = c32[...] + fr[0].astype(F32) + fr[1].astype(F32) + fr[2].astype(F32)
+    fb16[...] = total.astype(BF16)
+    twin = remote(fb16, dr, gss.at[15], grs.at[15], dp=1 - dp)
+    twin.start()
+    twin.wait_recv()
+    gfin[rows_of(core, z), :] = (fb16[...].astype(F32) + dr[...].astype(F32)).astype(BF16)
+
+    back_far, back_near, across = [], [], []
+
+    def same(zz, s, device):
+        block = gfin.at[rows_of(core, zz), :]
+        copy = remote(block, block, gss.at[s], grs.at[s], table=device)
+        copy.start()
+        return copy
+
+    def hand_on(zz, s):
+        for i in range(3):
+            back_near.append(same(zz, 19 + 3 * s + i, around(near_by[i])))
+        across.append(same(zz, 31 + s, sibling))
+
+    for s in range(3):
+        back_far.append(same(z, 16 + s, around(2 * steps[s])))
+    hand_on(z, 3)
+
     for copy in terms:
         copy.wait_recv()
 
@@ -277,52 +328,42 @@
         return carry
 
     lax.fori_loop(0, TENSOR, finish, 0)
-    for copy in far:
-        copy.wait_recv()
-    total = c32[chunk_rows(z), :] + fr[0].astype(F32) + fr[1].astype(F32) + fr[2].astype(F32)
-    fb16[...] = total.astype(BF16)
-    twin = remote(fb16, dr, gss.at[7], grs.at[7], dp=1 - dp)
-    twin.start()
-    twin.wait_recv()
-
-    base = HALF * core + CLASS * lax.rem(z, 4)
-    own_chunk = gfin.at[pl.ds(pl.multiple_of(base + CHUNK * (z // 4), 16), CHUNK), :]
-    own_chunk[...] = (fb16[...].astype(F32) + dr[...].astype(F32)).astype(BF16)
-    back_far = []
-    for i, k in enumerate((8, 4, 12)):
-        copy = remote(own_chunk, own_chunk, gss.at[8 + i], grs.at[8 + i], table=around(2 * k))
-        copy.start()
-        back_far.append(copy)
-    for copy in back_far:
-        copy.wait_recv()
-    own_class = gfin.at[pl.ds(pl.multiple_of(base, 16), CLASS), :]
-    back_near = []
-    for i in range(3):
-        copy = remote(own_class, own_class, gss.at[11 + i], grs.at[11 + i], table=around(near_by[i]))
-        copy.start()
-        back_near.append(copy)
-    across = [remote(own_class, own_class, gss.at[14], grs.at[14], table=sibling)]
-    across[0].start()
-    for i in range(3):
-        back_near[i].wait_recv()
-        q = z + Z - near_z[i]
-        block = gfin.at[pl.ds(pl.multiple_of(HALF * core + CLASS * lax.rem(q, 4), 16), CLASS), :]
-        copy = remote(block, block, gss.at[15 + i], grs.at[15 + i], table=sibling)
-        copy.start()
-        across.append(copy)
+    for s in (1, 2, 0):
+        back_far[s].wait_recv()
+        hand_on(z - steps[s], s)
+    for order, s in enumerate((3, 1, 2, 0)):
+        for i in range(3):
+            back_near[3 * order + i].wait_recv()
+            across.append(same(z - near_z[i] - steps[s], 35 + 3 * s + i, sibling))
     for copy in across:
         copy.wait_recv()
 
-    for t in range(4):
-        span = slice(128 * t, 128 * t + 128)
-        gu_ref[:, span] = gfin[512 * t : 512 * t + 512]
-        gd_ref[:, span] = gfin[2048 + 512 * t : 2560 + 512 * t]
-        gc_ref[:, span] = gfin[4096 + 64 * t : 4160 + 64 * t]
-    gb_ref[...] = gfin[4352:4416]
-
-    every = to_table + to_tensor + weights + sharps + [over] + gathers + [cores] + terms + near + far
+    every = to_table + to_tensor + weights + sharps + [over] + gathers + cores + terms + near + far
     for copy in every + [twin] + back_far + back_near + across:
         copy.wait_send()
+
+
+def write_out(mixed_ref, g_ref, mixed_hbm, gc_hbm, gb_hbm, gu_hbm, gd_hbm, gc, gb, gu, gd, sems):
+    copies = []
+
+    def send(ref, hbm):
+        copies.append(pltpu.make_async_copy(ref, hbm, sems.at[len(copies)]))
+        copies[-1].start()
+
+    send(mixed_ref, mixed_hbm)
+    for t in range(4):
+        gu[:, 128 * t : 128 * t + 128] = g_ref[512 * t : 512 * t + 512].astype(F32)
+    send(gu, gu_hbm)
+    for t in range(4):
+        gd[:, 128 * t : 128 * t + 128] = g_ref[2048 + 512 * t : 2560 + 512 * t].astype(F32)
+    send(gd, gd_hbm)
+    for t in range(4):
+        gc[:, 128 * t : 128 * t + 128] = g_ref[4096 + 64 * t : 4160 + 64 * t].astype(F32)
+    send(gc, gc_hbm)
+    gb[...] = g_ref[4352:4416].astype(F32).T[0:1]
+    send(gb, gb_hbm)
+    for copy in copies:
+        copy.wait()
 
 
 def body(
@@ -356,6 +397,15 @@
     )
     dma = pltpu.SemaphoreType.DMA
     scratch = [
+        pltpu.VMEM((128, 512), BF16),
+        pltpu.VMEM((1, 64), jnp.int32),
+        pltpu.VMEM((64, 64), F32),
+        pltpu.VMEM((1, 512), F32),
+        pltpu.VMEM((1, 64), F32),
+        pltpu.VMEM((1, 1), F32),
+        pltpu.VMEM((512, 512), BF16),
+        pltpu.VMEM((512, 512), BF16),
+        pltpu.VMEM((1024, 512), BF16),
         pltpu.VMEM((512, 128), BF16),
         pltpu.VMEM((32, 16, 128), BF16),
         pltpu.VMEM((32, 16, 128), F32),
@@ -378,37 +428,52 @@
         pltpu.VMEM((8, 64, 128), F32),
         pltpu.VMEM((ROWS, 128), F32),
         pltpu.VMEM((ROWS, 128), BF16),
-        pltpu.VMEM((HALF, 128), BF16),
-        pltpu.VMEM((HALF, 128), F32),
-        pltpu.VMEM((HALF, 128), BF16),
-        pltpu.VMEM((3, CLASS, 128), BF16),
-        pltpu.VMEM((CLASS, 128), F32),
-        pltpu.VMEM((CLASS, 128), BF16),
+        pltpu.VMEM((16, CHUNK, 128), BF16),
+        pltpu.VMEM((12, CHUNK, 128), BF16),
+        pltpu.VMEM((12, CHUNK, 128), BF16),
+        pltpu.VMEM((CHUNK, 128), F32),
+        pltpu.VMEM((3, CHUNK, 128), BF16),
         pltpu.VMEM((3, CHUNK, 128), BF16),
         pltpu.VMEM((CHUNK, 128), BF16),
         pltpu.VMEM((CHUNK, 128), BF16),
-        pltpu.VMEM((ROWS, 128), BF16),
     ]
-    for n in (32, 8, 8, 1, 8, 8, 8, 18):
+    for n in (32, 8, 8, 17, 8, 8, 8, 47):
         scratch += [dma((n,)), dma((n,))]
-    mixed, up, down, cross, bias = pl.pallas_call(
+    scratch.append(dma((12,)))
+    mixed, grads = pl.pallas_call(
         kernel,
         name="layer",
+        out_shape=(pltpu.VMEM((16, 64, 64), BF16), pltpu.VMEM((ROWS, 128), BF16)),
+        in_specs=[pl.BlockSpec(memory_space=pltpu.HBM)] * len(operands),
+        out_specs=(vmem,) * 2,
+        scratch_shapes=scratch,
+        compiler_params=pltpu.CompilerParams(
+            collective_id=0, has_side_effects=True, vmem_limit_bytes=58 * 2**20
+        ),
+    )(*operands)
+    hbm = pl.BlockSpec(memory_space=pltpu.HBM)
+    mixed, cross, bias, up, down = pl.pallas_call(
+        write_out,
+        name="write_out",
         out_shape=(
             jax.ShapeDtypeStruct((16, 64, 64), BF16),
-            jax.ShapeDtypeStruct((512, 512), BF16),
-            jax.ShapeDtypeStruct((512, 512), BF16),
-            jax.ShapeDtypeStruct((64, 512), BF16),
-            jax.ShapeDtypeStruct((64, 128), BF16),
+            jax.ShapeDtypeStruct((64, 512), F32),
+            jax.ShapeDtypeStruct((1, 64), F32),
+            jax.ShapeDtypeStruct((512, 512), F32),
+            jax.ShapeDtypeStruct((512, 512), F32),
         ),
-        in_specs=[vmem] * len(operands),
-        out_specs=(vmem,) * 5,
-        scratch_shapes=scratch,
-        compiler_params=pltpu.CompilerParams(
-            collective_id=0, has_side_effects=True, vmem_limit_bytes=48 * 2**20
-        ),
-    )(*operands)
-    return mixed, cross.astype(F32).T, bias[:, 0].astype(F32), up.astype(F32), down.astype(F32)
+        in_specs=(vmem,) * 2,
+        out_specs=(hbm,) * 5,
+        scratch_shapes=[
+            pltpu.VMEM((64, 512), F32),
+            pltpu.VMEM((1, 64), F32),
+            pltpu.VMEM((512, 512), F32),
+            pltpu.VMEM((512, 512), F32),
+            dma((5,)),
+        ],
+        compiler_params=pltpu.CompilerParams(vmem_limit_bytes=16 * 2**20),
+    )(mixed, grads)
+    return mixed, cross.T, bias.reshape(64), up, down
 
 
 def solution(mesh):

time: 116 us -> 101 us (0.87)
  local copies, waits for them, and re-layouts: 8.94 us -> 0 us
  other arithmetic: 3.49 us -> 0 us
  Pallas kernels: 102 us -> 98.9 us
    unnamed x23 -> x0, local copies, waits for them, and re-layouts: 8.94 us -> none
    pallas_call x1 -> x2, Pallas kernels: 102 us -> 98.9 us  [the longest x1 97.4 us: body(): pl.pallas_call(kernel, name='layer', out_shape=(pltpu.VMEM((16, 64, 64),...]
    convert_element_type x3 -> x0, other arithmetic: 2.82 us -> none  [the longest x1 1.1 us: body(): up.astype(F32)]
where the time goes in v2:
time: 101 us; the launch traced here: 100 us
  Pallas kernels  98.9 us (98%)
  between operations  1.29 us (1%)
    pallas_call x1, Pallas kernels, body(): pl.pallas_call(kernel, name='layer', out_shape=(pltpu.VMEM((16, 64, 64),...  97.4 us

profile of v2, /device:TPU:1, one launch (start us, length us, event | category | flops | bytes accessed | tf_op | source)
XLA Modules:
  0.0 100.2 jit_solution(6726899173166727583)
XLA Ops:
  1.3 97.4 %layer.1 = (bf16[16,64,64]{2,1,0:T(8,128)(2,1)S(1)}, bf16[4608,128]{1,0:T(8,128)(2,1)S(1)}) custom-call(bf16[128,512]{1,0:T(8,128)(2,1)} %bitcast.15, s32[1,64]{1,0:T(1,128)} %bitcast.18, f32[64,64]{1,0:T(8,128)} %shift_hbm.1, bf16[3,64,512]{2,1,0:T(8,128)(2,1)} %bitcast.14, f32[1,1]{1,0:T(1,128)} %bitcast.12.sharp_hbm, bf16[64,512]{1,0:T(8,128)(2,1)} %mex_hbm.1, ...), custom_call_target="tpu_custom_call" | custom-call | tf_op jit(solution)/shard_map/layer/pallas_call | solution.py:443
  98.7 1.5 %write_out.1 = (bf16[16,64,64]{2,1,0:T(8,128)(2,1)}, f32[64,512]{1,0:T(8,128)}, f32[1,64]{1,0:T(1,128)}, f32[512,512]{1,0:T(8,128)}, f32[512,512]{1,0:T(8,128)}) custom-call(bf16[16,64,64]{2,1,0:T(8,128)(2,1)S(1)} %get-tuple-element.12.mixed_ref, bf16[4608,128]{1,0:T(8,128)(2,1)S(1)} %get-tuple-element.13.g_ref), custom_call_target="tpu_custom_call" | custom-call | tf_op jit(solution)/shard_map/write_out/pallas_call | solution.py:455

commit v3 on v2

--- a/solution.py
+++ b/solution.py
@@ -16,6 +16,7 @@
 CLASS = 4 * CHUNK
 HALF = 4 * CLASS
 ROWS = 2 * HALF
+FAR_FIRST = [k for d in (8, 7, 9, 6, 10, 5, 11, 4, 12, 3, 13, 2, 14, 1, 15, 0) for k in (2 * d, 2 * d + 1) if k]
 
 
 def nn(a, b):
@@ -44,6 +45,26 @@
     g32, gb16, crecv, hb16, nr, c32, cb16, fr, fb16, dr,
     zss, zrs, tss, trs, wss, wrs, css, crs, sss, srs, ass, ars, mss, mrs, gss, grs, los,
 ):
+    dp = lax.axis_index("dp")
+    table = lax.axis_index("table")
+    tensor = lax.axis_index("tensor")
+    z, core = table // 2, lax.rem(table, 2)
+    hi, y = tensor // 4, lax.rem(tensor, 4)
+    sibling = table + 1 - 2 * core
+
+    def around(k):
+        return lax.rem(table + TABLE + k, TABLE)
+
+    def tensor_at(k):
+        return lax.rem(tensor + k, TENSOR)
+
+    barrier = pltpu.get_barrier_semaphore()
+    for k in FAR_FIRST:
+        pl.semaphore_signal(barrier, inc=1, device_id={"table": around(k)}, device_id_type=MESH)
+    for k in range(1, TENSOR):
+        pl.semaphore_signal(barrier, inc=1, device_id={"tensor": tensor_at(k)}, device_id_type=MESH)
+    pl.semaphore_signal(barrier, inc=1, device_id={"dp": 1 - dp}, device_id_type=MESH)
+
     loads = []
     for hbm, ref in (
         (f_hbm, f_ref), (wup_hbm, wup_ref), (wdn_hbm, wdn_ref), (int_hbm, low.at[0:64]), (cot_hbm, cot_ref),
@@ -53,25 +74,6 @@
         copy = pltpu.make_async_copy(hbm, ref, los.at[len(loads)])
         copy.start()
         loads.append(copy)
-    dp = lax.axis_index("dp")
-    table = lax.axis_index("table")
-    tensor = lax.axis_index("tensor")
-    z, core = table // 2, lax.rem(table, 2)
-    hi, y = tensor // 4, lax.rem(tensor, 4)
-    sibling = table + 1 - 2 * core
-
-    def around(k):
-        return lax.rem(table + TABLE + k, TABLE)
-
-    def tensor_at(k):
-        return lax.rem(tensor + k, TENSOR)
-
-    barrier = pltpu.get_barrier_semaphore()
-    for k in range(1, TABLE):
-        pl.semaphore_signal(barrier, inc=1, device_id={"table": around(k)}, device_id_type=MESH)
-    for k in range(1, TENSOR):
-        pl.semaphore_signal(barrier, inc=1, device_id={"tensor": tensor_at(k)}, device_id_type=MESH)
-    pl.semaphore_signal(barrier, inc=1, device_id={"dp": 1 - dp}, device_id_type=MESH)
 
     loads[0].wait()
     zs[...] = f_ref[...].T
@@ -103,29 +105,55 @@
 
     pl.semaphore_wait(barrier, TABLE - 1 + TENSOR - 1 + 1)
 
-    to_table = []
-    for d in (8, 7, 9, 6, 10, 5, 11, 4, 12, 3, 13, 2, 14, 1, 15, 0):
-        for k in (2 * d, 2 * d + 1):
-            if k == 0:
-                continue
-            rows = zs.at[pl.ds(pl.multiple_of(16 * around(k), 16), 16), :]
-            copy = remote(rows, arr.at[k - 1], zss.at[k], zrs.at[k], table=around(k))
-            copy.start()
-            to_table.append(copy)
-
-    pair = pl.ds(2 * core, 2)
-    mine = pl.ds(pl.multiple_of(64 * tensor, 64), 64)
-    all4[pair, mine, :] = own4[pair]
+    ring = (1, 3, 2)
+
+    def at(h, k):
+        return 4 * lax.rem(hi + h, 2) + lax.rem(y + 4 + k, 4)
+
+    def shard(block, count, owner):
+        return all4.at[pl.ds(2 * core + block, count), pl.ds(pl.multiple_of(64 * owner, 64), 64), :]
+
+    all4[pl.ds(2 * core, 2), pl.ds(pl.multiple_of(64 * tensor, 64), 64), :] = own4[pl.ds(2 * core, 2)]
     all_sharp[tensor] = own_sharp[...]
     weights, sharps = [], []
+
+    def spread(block, count, owner, n, to):
+        copy = remote(shard(block, count, owner), shard(block, count, owner), wss.at[n], wrs.at[n], tensor=to)
+        copy.start()
+        weights.append(copy)
+
+    spread(0, 2, tensor, 0, at(1, 0))
+    for k in ring:
+        spread(0, 2, tensor, k, at(0, k))
+
+    to_table = []
+    for k in FAR_FIRST:
+        rows = zs.at[pl.ds(pl.multiple_of(16 * around(k), 16), 16), :]
+        copy = remote(rows, arr.at[k - 1], zss.at[k], zrs.at[k], table=around(k))
+        copy.start()
+        to_table.append(copy)
     for k in range(1, TENSOR):
         copy = remote(own_sharp, all_sharp.at[tensor], sss.at[k], srs.at[k], tensor=tensor_at(k))
         copy.start()
         sharps.append(copy)
-    for k in range(1, TENSOR):
-        copy = remote(own4.at[pair], all4.at[pair, mine, :], wss.at[k], wrs.at[k], tensor=tensor_at(k))
-        copy.start()
-        weights.append(copy)
+
+    over = []
+
+    def hand_over(owner):
+        n = len(over)
+        copy = remote(shard(0, 2, owner), shard(0, 2, owner), css.at[n], crs.at[n], table=sibling)
+        copy.start()
+        over.append(copy)
+
+    hand_over(tensor)
+    weights[0].wait_recv()
+    for k in ring:
+        spread(0, 1, at(1, 0), 4 + k, at(0, k))
+    hand_over(at(1, 0))
+    for n, k in enumerate(ring):
+        weights[1 + n].wait_recv()
+        spread(1, 1, at(0, -k), 8 + k, at(1, 0))
+        hand_over(at(0, -k))
 
     for copy in to_table:
         copy.wait_recv()
@@ -152,10 +180,10 @@
     ctt[...] = term
     bias = jnp.sum(jnp.sum(term, axis=0), axis=1, keepdims=True)
 
-    for copy in weights:
-        copy.wait_recv()
-    over = remote(all4.at[pair], all4.at[pair], css.at[0], crs.at[0], table=sibling)
-    over.start()
+    for n, k in enumerate(ring):
+        weights[4 + n].wait_recv()
+        weights[7 + n].wait_recv()
+        hand_over(at(1, -k))
     for copy in to_tensor + sharps:
         copy.wait_recv()
 
@@ -164,7 +192,8 @@
         span = slice(128 * i, 128 * i + 128)
         xrow[0:64, span] = jnp.where(left, a, pltpu.roll(b, 64, 1)).astype(BF16)
         xrow[64:128, span] = jnp.where(left, pltpu.roll(a, 64, 1), b).astype(BF16)
-    over.wait_recv()
+    for copy in over:
+        copy.wait_recv()
 
     x = xrow[...]
     same_head = (iota((512, 512), 0) // 64 == iota((512, 512), 1) // 64).astype(F32).astype(BF16)
@@ -193,25 +222,37 @@
     mean = jnp.mean(summed * summed, axis=1, keepdims=True)
     nall[tensor] = (summed * lax.rsqrt(mean + EPS) * gain_ref[...]).astype(BF16)
 
-    def relative(r, sign):
-        dh, d = r // 4, lax.rem(r, 4)
-        dy = d + (d // 2) * (5 - 2 * d)
-        return 4 * lax.rem(hi + dh, 2) + lax.rem(y + 4 + sign * dy, 4)
-
-    gathers = []
-    for r in range(1, TENSOR):
-        copy = remote(nall.at[tensor], nall.at[tensor], ass.at[r], ars.at[r], tensor=relative(r, 1))
-        copy.start()
-        gathers.append(copy)
+    def pass_on(rows, n, to):
+        return remote(rows, rows, ass.at[n], ars.at[n], tensor=to)
+
+    pass_on(nall.at[tensor], 0, at(1, 0)).start()
+    for k in ring:
+        pass_on(nall.at[tensor], k, at(0, k)).start()
 
     off = jnp.sum(jnp.where(iota((64, 64), 0) == iota((64, 64), 1), off_ref[...], 0.0), axis=1, keepdims=True)
 
     def chunk(r, carry):
-        i = relative(r, -1)
-
-        @pl.when(r > 0)
+        m = lax.rem(r + 1, 3)
+        dy = (r + 6) // 8 * (1 + 2 * m - 3 * (m // 2))
+        dh = r // 5 + (r + 7) // 8 - (r + 6) // 8
+        i = at(dh, -dy)
+        first, second = nall.at[i, 0:64], nall.at[i, 64:128]
+
+        @pl.when(r == 1)
         def _():
-            remote(nall.at[i], nall.at[i], ass.at[r], ars.at[r], tensor=i).wait_recv()
+            pass_on(nall.at[i], 0, at(1, 0)).wait_recv()
+            for k in ring:
+                pass_on(first, 4 + k, at(0, k)).start()
+
+        @pl.when(jnp.logical_and(r >= 2, r <= 4))
+        def _():
+            pass_on(nall.at[i], dy, at(1, 0)).wait_recv()
+            pass_on(second, 8 + dy, at(1, 0)).start()
+
+        @pl.when(r >= 5)
+        def _():
+            pass_on(first, 4 + dy, at(1, 0)).wait_recv()
+            pass_on(second, 8 + dy, at(1, 0)).wait_recv()
 
         n = nall[i]
         h = nt(wup_t[...], n)
@@ -250,7 +291,7 @@
         for d in (1, -1, 2 - 4 * core, 0):
             n = len(cores)
             copy = remote(
-                gb16.at[rows_of(1 - core, z + d + k), :], crecv.at[n], css.at[1 + n], crs.at[1 + n], table=sibling
+                gb16.at[rows_of(1 - core, z + d + k), :], crecv.at[n], css.at[8 + n], crs.at[8 + n], table=sibling
             )
             copy.start()
             cores.append(copy)
@@ -338,9 +379,13 @@
     for copy in across:
         copy.wait_recv()
 
-    every = to_table + to_tensor + weights + sharps + [over] + gathers + cores + terms + near + far
-    for copy in every + [twin] + back_far + back_near + across:
+    for copy in to_table + to_tensor + weights + sharps + over + cores + terms + near + far + [twin] + back_far + back_near + across:
         copy.wait_send()
+    pass_on(nall.at[tensor], 0, at(1, 0)).wait_send()
+    for k in ring:
+        pass_on(nall.at[tensor], k, at(0, k)).wait_send()
+        pass_on(nall.at[tensor, 0:64], 4 + k, at(0, k)).wait_send()
+        pass_on(nall.at[tensor, 64:128], 8 + k, at(1, 0)).wait_send()
 
 
 def write_out(mixed_ref, g_ref, mixed_hbm, gc_hbm, gb_hbm, gu_hbm, gd_hbm, gc, gb, gu, gd, sems):
@@ -437,7 +482,7 @@
         pltpu.VMEM((CHUNK, 128), BF16),
         pltpu.VMEM((CHUNK, 128), BF16),
     ]
-    for n in (32, 8, 8, 17, 8, 8, 8, 47):
+    for n in (32, 8, 12, 24, 8, 12, 8, 47):
         scratch += [dma((n,)), dma((n,))]
     scratch.append(dma((12,)))
     mixed, grads = pl.pallas_call(

time: 101 us -> 92.5 us (0.916)
  Pallas kernels: 98.9 us -> 91.1 us
    pallas_call x1, Pallas kernels: 97.4 us -> 89.6 us  [body(): pl.pallas_call(kernel, name='layer', out_shape=(pltpu.VMEM((16, 64, 64),...]
where the time goes in v3:
time: 92.5 us; the launch traced here: 92.4 us
  Pallas kernels  91.1 us (98%)
  between operations  1.29 us (1%)
    pallas_call x1, Pallas kernels, body(): pl.pallas_call(kernel, name='layer', out_shape=(pltpu.VMEM((16, 64, 64),...  89.6 us

profile of v3, /device:TPU:1, one launch (start us, length us, event | category | flops | bytes accessed | tf_op | source)
XLA Modules:
  0.0 92.4 jit_solution(7113192499838536950)
XLA Ops:
  1.3 89.6 %layer.1 = (bf16[16,64,64]{2,1,0:T(8,128)(2,1)S(1)}, bf16[4608,128]{1,0:T(8,128)(2,1)S(1)}) custom-call(bf16[128,512]{1,0:T(8,128)(2,1)} %bitcast.15, s32[1,64]{1,0:T(1,128)} %bitcast.18, f32[64,64]{1,0:T(8,128)} %shift_hbm.1, bf16[3,64,512]{2,1,0:T(8,128)(2,1)} %bitcast.14, f32[1,1]{1,0:T(1,128)} %bitcast.12.sharp_hbm, bf16[64,512]{1,0:T(8,128)(2,1)} %mex_hbm.1, ...), custom_call_target="tpu_custom_call" | custom-call | tf_op jit(solution)/shard_map/layer/pallas_call | solution.py:488
  90.9 1.5 %write_out.1 = (bf16[16,64,64]{2,1,0:T(8,128)(2,1)}, f32[64,512]{1,0:T(8,128)}, f32[1,64]{1,0:T(1,128)}, f32[512,512]{1,0:T(8,128)}, f32[512,512]{1,0:T(8,128)}) custom-call(bf16[16,64,64]{2,1,0:T(8,128)(2,1)S(1)} %get-tuple-element.12.mixed_ref, bf16[4608,128]{1,0:T(8,128)(2,1)S(1)} %get-tuple-element.13.g_ref), custom_call_target="tpu_custom_call" | custom-call | tf_op jit(solution)/shard_map/write_out/pallas_call | solution.py:500

commit v4 on v3

--- a/solution.py
+++ b/solution.py
@@ -12,7 +12,8 @@
 EPS = 1e-06
 
 TABLE, TENSOR, Z = 32, 8, 16
-CHUNK = 144
+PIECE = 80
+CHUNK = 2 * PIECE
 CLASS = 4 * CHUNK
 HALF = 4 * CLASS
 ROWS = 2 * HALF
@@ -41,9 +42,9 @@
     f_hbm, pos_hbm, shift_hbm, wqkv_hbm, sharp_hbm, mex_hbm, gain_hbm, int_hbm, off_hbm, wup_hbm, wdn_hbm, cot_hbm,
     mixed_ref, gfin,
     f_ref, pos_ref, shift_ref, gain_ref, off_ref, sharp_ref, wup_ref, wdn_ref, cot_ref,
-    zs, arr, arrf, xin, xa, own4, all4, own_sharp, all_sharp, xrow, nall, back, wup_t, wdn_t, low, xt, ctt, mlp, rs, cross,
-    g32, gb16, crecv, hb16, nr, c32, cb16, fr, fb16, dr,
-    zss, zrs, tss, trs, wss, wrs, css, crs, sss, srs, ass, ars, mss, mrs, gss, grs, los,
+    zs, arr, arrf, xin, xa, own4, all4, own_sharp, all_sharp, xrow, nall, back, wup_t, wdn_t, low, xt, ctt, mlp, rs, xs, xr, cross,
+    g32, gs16, crecv, db16, drecv, hb16, nr, cb16, fr,
+    zss, zrs, tss, trs, wss, wrs, css, crs, sss, srs, ass, ars, mss, mrs, gss, grs, dss, drs, oss, ors, los,
 ):
     dp = lax.axis_index("dp")
     table = lax.axis_index("table")
@@ -58,6 +59,11 @@
     def tensor_at(k):
         return lax.rem(tensor + k, TENSOR)
 
+    def settle(*groups):
+        for group in groups:
+            for copy in group:
+                copy.wait_send()
+
     barrier = pltpu.get_barrier_semaphore()
     for k in FAR_FIRST:
         pl.semaphore_signal(barrier, inc=1, device_id={"table": around(k)}, device_id_type=MESH)
@@ -67,9 +73,9 @@
 
     loads = []
     for hbm, ref in (
-        (f_hbm, f_ref), (wup_hbm, wup_ref), (wdn_hbm, wdn_ref), (int_hbm, low.at[0:64]), (cot_hbm, cot_ref),
-        (wqkv_hbm, own4.at[0:3]), (mex_hbm, own4.at[3]), (pos_hbm, pos_ref), (shift_hbm, shift_ref),
-        (gain_hbm, gain_ref), (off_hbm, off_ref), (sharp_hbm, sharp_ref),
+        (f_hbm, f_ref), (wqkv_hbm, own4.at[0:3]), (mex_hbm, own4.at[3]), (sharp_hbm, sharp_ref), (wup_hbm, wup_ref),
+        (wdn_hbm, wdn_ref), (int_hbm, low.at[0:64]), (cot_hbm, cot_ref), (pos_hbm, pos_ref), (shift_hbm, shift_ref),
+        (gain_hbm, gain_ref), (off_hbm, off_ref),
     ):
         copy = pltpu.make_async_copy(hbm, ref, los.at[len(loads)])
         copy.start()
@@ -78,19 +84,64 @@
     loads[0].wait()
     zs[...] = f_ref[...].T
     arr[TABLE - 1] = zs[pl.ds(pl.multiple_of(16 * table, 16), 16), :]
-    loads[1].wait()
-    wup_t[...] = wup_ref[...].T
-    loads[2].wait()
-    wdn_t[...] = wdn_ref[...].T
-    for copy in loads[3:]:
+    for copy in loads[1:4]:
         copy.wait()
     own_sharp[...] = jnp.broadcast_to(sharp_ref[...], own_sharp.shape)
+
+    pl.semaphore_wait(barrier, TABLE - 1 + TENSOR - 1 + 1)
+
+    ring = (1, 3, 2)
+
+    def at(h, k):
+        return 4 * lax.rem(hi + h, 2) + lax.rem(y + 4 + k, 4)
+
+    def shard(block, count, owner):
+        return all4.at[pl.ds(2 * core + block, count), pl.ds(pl.multiple_of(64 * owner, 64), 64), :]
+
+    all4[pl.ds(2 * core, 2), pl.ds(pl.multiple_of(64 * tensor, 64), 64), :] = own4[pl.ds(2 * core, 2)]
+    all_sharp[tensor] = own_sharp[...]
+    weights, sharps = [], []
+
+    def spread(block, count, owner, n, to):
+        copy = remote(shard(block, count, owner), shard(block, count, owner), wss.at[n], wrs.at[n], tensor=to)
+        copy.start()
+        weights.append(copy)
+
+    spread(0, 2, tensor, 0, at(1, 0))
+    for k in ring:
+        spread(0, 2, tensor, k, at(0, k))
+
+    for k in FAR_FIRST:
+        rows = zs.at[pl.ds(pl.multiple_of(16 * around(k), 16), 16), :]
+        remote(rows, arr.at[k - 1], zss.at[0], zrs.at[0], table=around(k)).start()
+    all_rows = remote(arr.at[0 : TABLE - 1], arr.at[0 : TABLE - 1], zss.at[0], zrs.at[0], table=around(1))
+    for k in range(1, TENSOR):
+        copy = remote(own_sharp, all_sharp.at[tensor], sss.at[k], srs.at[k], tensor=tensor_at(k))
+        copy.start()
+        sharps.append(copy)
+
+    over = []
+
+    def hand_over(owner):
+        n = len(over)
+        copy = remote(shard(0, 2, owner), shard(0, 2, owner), css.at[n], crs.at[n], table=sibling)
+        copy.start()
+        over.append(copy)
+
+    hand_over(tensor)
+
+    for copy in loads[4:]:
+        copy.wait()
+    wup_t[...] = wup_ref[...].T
+    wdn_t[...] = wdn_ref[...].T
     low[64:128] = (iota((64, 512), 1) == 64 * tensor + iota((64, 512), 0)).astype(F32).astype(BF16)
+
     def backward(i, carry):
         rows = cot_ref[pl.ds(pl.multiple_of(128 * i, 128), 128), :]
         back[i] = nt(wdn_ref[...], rows)
         ctt[i] = nt(low[64:128], rows)
         return carry
+
     lax.fori_loop(0, TENSOR, backward, 0)
     g32[...] = jnp.zeros_like(g32)
 
@@ -103,49 +154,6 @@
     shift = shift_ref[...]
     shift = jnp.concatenate([shift, shift], axis=1)
 
-    pl.semaphore_wait(barrier, TABLE - 1 + TENSOR - 1 + 1)
-
-    ring = (1, 3, 2)
-
-    def at(h, k):
-        return 4 * lax.rem(hi + h, 2) + lax.rem(y + 4 + k, 4)
-
-    def shard(block, count, owner):
-        return all4.at[pl.ds(2 * core + block, count), pl.ds(pl.multiple_of(64 * owner, 64), 64), :]
-
-    all4[pl.ds(2 * core, 2), pl.ds(pl.multiple_of(64 * tensor, 64), 64), :] = own4[pl.ds(2 * core, 2)]
-    all_sharp[tensor] = own_sharp[...]
-    weights, sharps = [], []
-
-    def spread(block, count, owner, n, to):
-        copy = remote(shard(block, count, owner), shard(block, count, owner), wss.at[n], wrs.at[n], tensor=to)
-        copy.start()
-        weights.append(copy)
-
-    spread(0, 2, tensor, 0, at(1, 0))
-    for k in ring:
-        spread(0, 2, tensor, k, at(0, k))
-
-    to_table = []
-    for k in FAR_FIRST:
-        rows = zs.at[pl.ds(pl.multiple_of(16 * around(k), 16), 16), :]
-        copy = remote(rows, arr.at[k - 1], zss.at[k], zrs.at[k], table=around(k))
-        copy.start()
-        to_table.append(copy)
-    for k in range(1, TENSOR):
-        copy = remote(own_sharp, all_sharp.at[tensor], sss.at[k], srs.at[k], tensor=tensor_at(k))
-        copy.start()
-        sharps.append(copy)
-
-    over = []
-
-    def hand_over(owner):
-        n = len(over)
-        copy = remote(shard(0, 2, owner), shard(0, 2, owner), css.at[n], crs.at[n], table=sibling)
-        copy.start()
-        over.append(copy)
-
-    hand_over(tensor)
     weights[0].wait_recv()
     for k in ring:
         spread(0, 1, at(1, 0), 4 + k, at(0, k))
@@ -155,8 +163,7 @@
         spread(1, 1, at(0, -k), 8 + k, at(1, 0))
         hand_over(at(0, -k))
 
-    for copy in to_table:
-        copy.wait_recv()
+    all_rows.wait_recv()
     arrf[...] = arr[...].astype(F32)
     for i in range(TENSOR):
         a, b = arrf[:, 2 * i, :], arrf[:, 2 * i + 1, :]
@@ -229,6 +236,7 @@
     for k in ring:
         pass_on(nall.at[tensor], k, at(0, k)).start()
 
+    settle([all_rows], to_tensor, weights, sharps, over)
     off = jnp.sum(jnp.where(iota((64, 64), 0) == iota((64, 64), 1), off_ref[...], 0.0), axis=1, keepdims=True)
 
     def chunk(r, carry):
@@ -276,116 +284,177 @@
     lax.fori_loop(0, TENSOR, chunk, 0)
     g32[4352:4416] = jnp.broadcast_to(bias, (64, 128))
 
-    gb16[...] = g32[...].astype(BF16)
-
-    def owned(zz):
+    def rows_of(c, zz, d, count):
         zz = lax.rem(zz + 2 * Z, Z)
-        return pl.multiple_of(CLASS * lax.rem(zz, 4) + CHUNK * (zz // 4), 16)
-
-    def rows_of(c, zz):
-        return pl.ds(pl.multiple_of(HALF * c + owned(zz), 16), CHUNK)
+        start = HALF * c + CLASS * lax.rem(zz, 4) + CHUNK * (zz // 4) + PIECE * d
+        return pl.ds(pl.multiple_of(start, 16), count)
+
+    def half(d):
+        return pl.ds(pl.multiple_of(PIECE * d, 16), PIECE)
 
     steps = (8, 4, 12, 0)
-    cores = []
-    for k in steps:
-        for d in (1, -1, 2 - 4 * core, 0):
-            n = len(cores)
+    near_z = (1, -1, 4 * core - 2)
+    near_by = (2, -2, 8 * core - 4)
+    cores, twins, near, far = [], [], [], []
+    for s, k in enumerate(steps):
+        for j, d in enumerate((1, -1, 2 - 4 * core, 0)):
+            gs16[4 * s + j] = g32[rows_of(1 - core, z + d + k, 0, CHUNK), :].astype(BF16)
+        four = pl.ds(4 * s, 4)
+        copy = remote(gs16.at[four], crecv.at[four], css.at[8 + s], crs.at[8 + s], table=sibling)
+        copy.start()
+        cores.append(copy)
+
+    def columns_of(h, k):
+        return pl.ds(pl.multiple_of(64 * at(h, k), 64), 64)
+
+    terms = []
+    for n, k in enumerate(ring):
+        for h in range(2):
             copy = remote(
-                gb16.at[rows_of(1 - core, z + d + k), :], crecv.at[n], css.at[8 + n], crs.at[8 + n], table=sibling
+                mlp.at[:, columns_of(h, k), :], rs.at[2 * n + h], mss.at[2 * n + h], mrs.at[2 * n + h], tensor=at(0, k)
             )
             copy.start()
-            cores.append(copy)
-    terms = []
-    for k in range(1, TENSOR):
-        to = tensor_at(k)
-        rows = mlp.at[:, pl.ds(pl.multiple_of(64 * to, 64), 64), :]
-        copy = remote(rows, rs.at[k - 1], mss.at[k], mrs.at[k], tensor=to)
-        copy.start()
-        terms.append(copy)
-
-    near_z = (1, -1, 4 * core - 2)
-    near_by = (2, -2, 8 * core - 4)
-    near = []
+            terms.append(copy)
+
     for s, k in enumerate(steps):
+        cores[s].wait_recv()
+        for j, d in enumerate(near_z + (0,)):
+            n = 4 * s + j
+            theirs = g32[rows_of(core, z + d + k, 1 - dp, PIECE), :] + crecv[n, half(1 - dp), :].astype(F32)
+            db16[n] = theirs.astype(BF16)
+        four = pl.ds(4 * s, 4)
+        copy = remote(db16.at[four], drecv.at[four], dss.at[s], drs.at[s], dp=1 - dp)
+        copy.start()
+        twins.append(copy)
+
+    def ours(n, zz):
+        total = g32[rows_of(core, zz, dp, PIECE), :] + crecv[n, half(dp), :].astype(F32)
+        return total + drecv[n].astype(F32)
+
+    def send_near(s):
+        twins[s].wait_recv()
         for i in range(3):
-            n = 4 * s + i
-            cores[n].wait_recv()
-            part = g32[rows_of(core, z + near_z[i] + k), :] + crecv[n].astype(F32)
-            hb16[3 * s + i] = part.astype(BF16)
-            copy = remote(hb16.at[3 * s + i], nr.at[3 * s + i], gss.at[3 * s + i], grs.at[3 * s + i], table=around(near_by[i]))
+            n = 3 * s + i
+            hb16[n] = ours(4 * s + i, z + near_z[i] + steps[s]).astype(BF16)
+            copy = remote(hb16.at[n], nr.at[n], gss.at[n], grs.at[n], table=around(near_by[i]))
             copy.start()
             near.append(copy)
-    far = []
-    for s, k in enumerate(steps):
-        n = 4 * s + 3
-        cores[n].wait_recv()
-        total = g32[rows_of(core, z + k), :] + crecv[n].astype(F32)
-        for i in range(3):
-            near[3 * s + i].wait_recv()
-            total = total + nr[3 * s + i].astype(F32)
-        if k:
-            cb16[s] = total.astype(BF16)
-            copy = remote(cb16.at[s], fr.at[s], gss.at[12 + s], grs.at[12 + s], table=around(2 * k))
-            copy.start()
-            far.append(copy)
-        else:
-            c32[...] = total
-    for copy in far:
-        copy.wait_recv()
-    total = c32[...] + fr[0].astype(F32) + fr[1].astype(F32) + fr[2].astype(F32)
-    fb16[...] = total.astype(BF16)
-    twin = remote(fb16, dr, gss.at[15], grs.at[15], dp=1 - dp)
-    twin.start()
-    twin.wait_recv()
-    gfin[rows_of(core, z), :] = (fb16[...].astype(F32) + dr[...].astype(F32)).astype(BF16)
-
-    back_far, back_near, across = [], [], []
-
-    def same(zz, s, device):
-        block = gfin.at[rows_of(core, zz), :]
-        copy = remote(block, block, gss.at[s], grs.at[s], table=device)
-        copy.start()
-        return copy
-
-    def hand_on(zz, s):
-        for i in range(3):
-            back_near.append(same(zz, 19 + 3 * s + i, around(near_by[i])))
-        across.append(same(zz, 31 + s, sibling))
-
-    for s in range(3):
-        back_far.append(same(z, 16 + s, around(2 * steps[s])))
-    hand_on(z, 3)
-
+
+    def four_chips(s):
+        total = ours(4 * s + 3, z + steps[s])
+        for n in range(3 * s, 3 * s + 3):
+            near[n].wait_recv()
+            total = total + nr[n].astype(F32)
+        return total
+
+    def send_far(s):
+        cb16[s] = four_chips(s).astype(BF16)
+        copy = remote(cb16.at[s], fr.at[s], gss.at[12 + s], grs.at[12 + s], table=around(2 * steps[s]))
+        copy.start()
+        far.append(copy)
+
+    send_near(0)
+    send_near(1)
+    send_far(0)
+    send_near(2)
+    send_far(1)
+    send_near(3)
+    send_far(2)
     for copy in terms:
         copy.wait_recv()
 
-    def finish(i, carry):
-        own = mlp[i, pl.ds(pl.multiple_of(64 * tensor, 64), 64), :].astype(F32)
-        for k in range(1, TENSOR):
-            own = own + rs[k - 1, i].astype(F32)
-        out = (cross[i] + own).T
-        mixed_ref[2 * i] = out[0:64].astype(BF16)
-        mixed_ref[2 * i + 1] = out[64:128].astype(BF16)
+    def term_sum(i, h):
+        total = mlp[i, columns_of(h, 0), :].astype(F32)
+        for n in range(3):
+            total = total + rs[2 * n + h, i].astype(F32)
+        return total
+
+    def partner_terms(i, carry):
+        xs[i] = term_sum(i, 1).astype(BF16)
         return carry
 
-    lax.fori_loop(0, TENSOR, finish, 0)
-    for s in (1, 2, 0):
-        back_far[s].wait_recv()
-        hand_on(z - steps[s], s)
-    for order, s in enumerate((3, 1, 2, 0)):
+    lax.fori_loop(0, TENSOR, partner_terms, 0)
+    terms.append(remote(xs, xr, mss.at[6], mrs.at[6], tensor=at(1, 0)))
+    terms[6].start()
+    total = four_chips(3)
+    for n, copy in enumerate(far):
+        copy.wait_recv()
+        total = total + fr[n].astype(F32)
+    gfin[rows_of(core, z, dp, PIECE), :] = total.astype(BF16)
+
+    back_far, back_near, back_dp, across = {}, {}, {}, {}
+
+    def same(zz, send, recv, n, **device):
+        block = gfin.at[rows_of(core, zz, dp, PIECE), :]
+        copy = remote(block, block, send.at[n], recv.at[n], **device)
+        copy.start()
+        return copy
+
+    def owner(s, i):
+        return z - steps[s] - (near_z + (0,))[i]
+
+    def to_dp(s, i):
+        back_dp[s, i] = same(owner(s, i), dss, drs, 16 + 4 * s + i, dp=1 - dp)
+
+    def to_near(s):
         for i in range(3):
-            back_near[3 * order + i].wait_recv()
-            across.append(same(z - near_z[i] - steps[s], 35 + 3 * s + i, sibling))
-    for copy in across:
-        copy.wait_recv()
-
-    for copy in to_table + to_tensor + weights + sharps + over + cores + terms + near + far + [twin] + back_far + back_near + across:
-        copy.wait_send()
+            back_near[s, i] = same(owner(s, 3), gss, grs, 18 + 3 * s + i, table=around(near_by[i]))
+
+    def to_core(s, i):
+        back_dp[s, i].wait_recv()
+        block = gfin.at[rows_of(core, owner(s, i), 0, CHUNK), :]
+        across[s, i] = remote(block, block, oss.at[4 * s + i], ors.at[4 * s + i], table=sibling)
+        across[s, i].start()
+
+    def from_near(s):
+        for i in range(3):
+            back_near[s, i].wait_recv()
+            to_dp(s, i)
+
+    for s in range(3):
+        back_far[s] = same(z, gss, grs, 15 + s, table=around(2 * steps[s]))
+    to_near(3)
+    to_dp(3, 3)
+    settle(cores, twins, near, far, terms[:6])
     pass_on(nall.at[tensor], 0, at(1, 0)).wait_send()
     for k in ring:
         pass_on(nall.at[tensor], k, at(0, k)).wait_send()
         pass_on(nall.at[tensor, 0:64], 4 + k, at(0, k)).wait_send()
         pass_on(nall.at[tensor, 64:128], 8 + k, at(1, 0)).wait_send()
+    from_near(3)
+    to_core(3, 3)
+    for s in (1, 2):
+        back_far[s].wait_recv()
+        to_near(s)
+        to_dp(s, 3)
+    for i in range(3):
+        to_core(3, i)
+    back_far[0].wait_recv()
+    to_near(0)
+    to_dp(0, 3)
+    from_near(1)
+    from_near(2)
+
+    terms[6].wait_recv()
+
+    def finish(i, carry):
+        own = term_sum(i, 0) + xr[i].astype(F32)
+        out = (cross[i] + own).T
+        mixed_ref[2 * i] = out[0:64].astype(BF16)
+        mixed_ref[2 * i + 1] = out[64:128].astype(BF16)
+        return carry
+
+    lax.fori_loop(0, TENSOR, finish, 0)
+    from_near(0)
+    for s in (1, 2):
+        for i in (3, 0, 1, 2):
+            to_core(s, i)
+    for i in (3, 0, 1, 2):
+        to_core(0, i)
+    settle(terms[6:], back_far.values(), back_near.values(), back_dp.values())
+    for copy in across.values():
+        copy.wait_recv()
+    settle(across.values())
 
 
 def write_out(mixed_ref, g_ref, mixed_hbm, gc_hbm, gb_hbm, gu_hbm, gd_hbm, gc, gb, gu, gd, sems):
@@ -469,20 +538,21 @@
         pltpu.VMEM((8, 64, 128), F32),
         pltpu.VMEM((8, 64, 128), F32),
         pltpu.VMEM((8, 512, 128), BF16),
-        pltpu.VMEM((7, 8, 64, 128), BF16),
+        pltpu.VMEM((6, 8, 64, 128), BF16),
+        pltpu.VMEM((8, 64, 128), BF16),
+        pltpu.VMEM((8, 64, 128), BF16),
         pltpu.VMEM((8, 64, 128), F32),
         pltpu.VMEM((ROWS, 128), F32),
-        pltpu.VMEM((ROWS, 128), BF16),
         pltpu.VMEM((16, CHUNK, 128), BF16),
-        pltpu.VMEM((12, CHUNK, 128), BF16),
-        pltpu.VMEM((12, CHUNK, 128), BF16),
-        pltpu.VMEM((CHUNK, 128), F32),
-        pltpu.VMEM((3, CHUNK, 128), BF16),
-        pltpu.VMEM((3, CHUNK, 128), BF16),
-        pltpu.VMEM((CHUNK, 128), BF16),
-        pltpu.VMEM((CHUNK, 128), BF16),
+        pltpu.VMEM((16, CHUNK, 128), BF16),
+        pltpu.VMEM((16, PIECE, 128), BF16),
+        pltpu.VMEM((16, PIECE, 128), BF16),
+        pltpu.VMEM((12, PIECE, 128), BF16),
+        pltpu.VMEM((12, PIECE, 128), BF16),
+        pltpu.VMEM((3, PIECE, 128), BF16),
+        pltpu.VMEM((3, PIECE, 128), BF16),
     ]
-    for n in (32, 8, 12, 24, 8, 12, 8, 47):
+    for n in (1, 8, 12, 12, 8, 12, 7, 30, 32, 16):
         scratch += [dma((n,)), dma((n,))]
     scratch.append(dma((12,)))
     mixed, grads = pl.pallas_call(

time: 92.5 us -> 89.6 us (0.969)
  Pallas kernels: 91.1 us -> 88.2 us
    pallas_call x1, Pallas kernels: 89.6 us -> 86.6 us  [body(): pl.pallas_call(kernel, name='layer', out_shape=(pltpu.VMEM((16, 64, 64),...]
where the time goes in v4:
time: 89.6 us; the launch traced here: 89.5 us
  Pallas kernels  88.2 us (98%)
  between operations  1.29 us (1%)
    pallas_call x1, Pallas kernels, body(): pl.pallas_call(kernel, name='layer', out_shape=(pltpu.VMEM((16, 64, 64),...  86.6 us

profile of v4, /device:TPU:1, one launch (start us, length us, event | category | flops | bytes accessed | tf_op | source)
XLA Modules:
  0.0 89.5 jit_solution(13053578503154802747)
XLA Ops:
  1.3 86.6 %layer.1 = (bf16[16,64,64]{2,1,0:T(8,128)(2,1)S(1)}, bf16[5120,128]{1,0:T(8,128)(2,1)S(1)}) custom-call(bf16[128,512]{1,0:T(8,128)(2,1)} %bitcast.15, s32[1,64]{1,0:T(1,128)} %bitcast.18, f32[64,64]{1,0:T(8,128)} %shift_hbm.1, bf16[3,64,512]{2,1,0:T(8,128)(2,1)} %bitcast.14, f32[1,1]{1,0:T(1,128)} %bitcast.12.sharp_hbm, bf16[64,512]{1,0:T(8,128)(2,1)} %mex_hbm.1, ...), custom_call_target="tpu_custom_call" | custom-call | tf_op jit(solution)/shard_map/layer/pallas_call | solution.py:558
  87.9 1.5 %write_out.1 = (bf16[16,64,64]{2,1,0:T(8,128)(2,1)}, f32[64,512]{1,0:T(8,128)}, f32[1,64]{1,0:T(1,128)}, f32[512,512]{1,0:T(8,128)}, f32[512,512]{1,0:T(8,128)}) custom-call(bf16[16,64,64]{2,1,0:T(8,128)(2,1)S(1)} %get-tuple-element.12.mixed_ref, bf16[5120,128]{1,0:T(8,128)(2,1)S(1)} %get-tuple-element.13.g_ref), custom_call_target="tpu_custom_call" | custom-call | tf_op jit(solution)/shard_map/write_out/pallas_call | solution.py:570

commit v5 on v4

--- a/solution.py
+++ b/solution.py
@@ -203,28 +203,27 @@
         copy.wait_recv()
 
     x = xrow[...]
-    same_head = (iota((512, 512), 0) // 64 == iota((512, 512), 1) // 64).astype(F32).astype(BF16)
-
-    def unit(v):
-        squares = nn((v * v).astype(BF16), same_head)
-        return v * lax.rsqrt(squares * (1.0 / 64) + EPS)
-
-    query = unit(nt(x, all4[0]))
-    key = unit(nt(x, all4[1])).astype(BF16)
-    value = nt(x, all4[2])
-    same_sample = iota((128, 128), 0) // 64 == iota((128, 128), 1) // 64
+    spans = [slice(128 * i, 128 * i + 128) for i in range(4)]
+    same = iota((128, 128), 0) // 64 == iota((128, 128), 1) // 64
+    same_head = same.astype(F32).astype(BF16)
+    query, key, value = nt(x, all4[0]), nt(x, all4[1]), nt(x, all4[2])
+    pairs = jnp.concatenate([query[:, span] for span in spans] + [key[:, span] for span in spans], axis=0)
+    pairs = pairs * lax.rsqrt(nn((pairs * pairs).astype(BF16), same_head) * (1.0 / 64) + EPS)
+    ones = jnp.concatenate([jnp.where(left, 1.0, jnp.zeros((128, 128), F32)), jnp.where(left, jnp.zeros((128, 128), F32), 1.0)], axis=0)
     heads = []
     for i in range(4):
-        span = slice(128 * i, 128 * i + 128)
-        q, k, v = query[:, span], key[:, span], value[:, span]
-        parts = []
-        for s in range(2):
-            half = left if s == 0 else jnp.logical_not(left)
-            scores = nt(jnp.where(half, q, 0.0).astype(BF16), k) * (all_sharp[2 * i + s, 0:1, :] * (1.0 / 64))
-            e = jnp.where(same_sample, jnp.exp(scores), 0.0).astype(BF16)
-            o = nn(e, jnp.where(half, v, 1.0).astype(BF16))
-            parts.append(o / pltpu.roll(o, 64, 1))
-        heads.append(jnp.where(left, parts[0], parts[1]).astype(BF16))
+        q, k = pairs[128 * i : 128 * i + 128], pairs[512 + 128 * i : 640 + 128 * i].astype(BF16)
+        both = jnp.concatenate([jnp.where(left, q, 0.0), jnp.where(left, 0.0, q)], axis=0).astype(BF16)
+        scores = nt(both, k)
+        e = [
+            jnp.where(same, jnp.exp(scores[128 * s : 128 * s + 128] * (all_sharp[2 * i + s, 0:1, :] * (1.0 / 64))), 0.0)
+            for s in range(2)
+        ]
+        v = value[:, spans[i]]
+        v = jnp.concatenate([jnp.where(left, v, 0.0), jnp.where(left, 0.0, v)], axis=0)
+        v = jnp.concatenate([v, ones], axis=1).astype(BF16)
+        o = nn(jnp.concatenate(e, axis=1).astype(BF16), v)
+        heads.append((o[:, 0:128] / o[:, 128:256]).astype(BF16))
     summed = nn(jnp.concatenate(heads, axis=1), all4[3]) + x.astype(F32)
     mean = jnp.mean(summed * summed, axis=1, keepdims=True)
     nall[tensor] = (summed * lax.rsqrt(mean + EPS) * gain_ref[...]).astype(BF16)
@@ -384,7 +383,7 @@
 
     back_far, back_near, back_dp, across = {}, {}, {}, {}
 
-    def same(zz, send, recv, n, **device):
+    def send_same(zz, send, recv, n, **device):
         block = gfin.at[rows_of(core, zz, dp, PIECE), :]
         copy = remote(block, block, send.at[n], recv.at[n], **device)
         copy.start()
@@ -394,11 +393,11 @@
         return z - steps[s] - (near_z + (0,))[i]
 
     def to_dp(s, i):
-        back_dp[s, i] = same(owner(s, i), dss, drs, 16 + 4 * s + i, dp=1 - dp)
+        back_dp[s, i] = send_same(owner(s, i), dss, drs, 16 + 4 * s + i, dp=1 - dp)
 
     def to_near(s):
         for i in range(3):
-            back_near[s, i] = same(owner(s, 3), gss, grs, 18 + 3 * s + i, table=around(near_by[i]))
+            back_near[s, i] = send_same(owner(s, 3), gss, grs, 18 + 3 * s + i, table=around(near_by[i]))
 
     def to_core(s, i):
         back_dp[s, i].wait_recv()
@@ -412,7 +411,7 @@
             to_dp(s, i)
 
     for s in range(3):
-        back_far[s] = same(z, gss, grs, 15 + s, table=around(2 * steps[s]))
+        back_far[s] = send_same(z, gss, grs, 15 + s, table=around(2 * steps[s]))
     to_near(3)
     to_dp(3, 3)
     settle(cores, twins, near, far, terms[:6])

time: 89.6 us -> 88.9 us (level)
  no operation moved by 1% of the time
where the time goes in v5:
time: 88.9 us; the launch traced here: 88.8 us
  Pallas kernels  87.5 us (98%)
  between operations  1.29 us (1%)
    pallas_call x1, Pallas kernels, body(): pl.pallas_call(kernel, name='layer', out_shape=(pltpu.VMEM((16, 64, 64),...  86 us

profile of v5, /device:TPU:1, one launch (start us, length us, event | category | flops | bytes accessed | tf_op | source)
XLA Modules:
  0.0 88.8 jit_solution(12880626407026857945)
XLA Ops:
  1.3 86.0 %layer.1 = (bf16[16,64,64]{2,1,0:T(8,128)(2,1)S(1)}, bf16[5120,128]{1,0:T(8,128)(2,1)S(1)}) custom-call(bf16[128,512]{1,0:T(8,128)(2,1)} %bitcast.15, s32[1,64]{1,0:T(1,128)} %bitcast.18, f32[64,64]{1,0:T(8,128)} %shift_hbm.1, bf16[3,64,512]{2,1,0:T(8,128)(2,1)} %bitcast.14, f32[1,1]{1,0:T(1,128)} %bitcast.12.sharp_hbm, bf16[64,512]{1,0:T(8,128)(2,1)} %mex_hbm.1, ...), custom_call_target="tpu_custom_call" | custom-call | tf_op jit(solution)/shard_map/layer/pallas_call | solution.py:557
  87.3 1.5 %write_out.1 = (bf16[16,64,64]{2,1,0:T(8,128)(2,1)}, f32[64,512]{1,0:T(8,128)}, f32[1,64]{1,0:T(1,128)}, f32[512,512]{1,0:T(8,128)}, f32[512,512]{1,0:T(8,128)}) custom-call(bf16[16,64,64]{2,1,0:T(8,128)(2,1)S(1)} %get-tuple-element.12.mixed_ref, bf16[5120,128]{1,0:T(8,128)(2,1)S(1)} %get-tuple-element.13.g_ref), custom_call_target="tpu_custom_call" | custom-call | tf_op jit(solution)/shard_map/write_out/pallas_call | solution.py:569

commit v6 on v5

--- a/solution.py
+++ b/solution.py
@@ -43,7 +43,7 @@
     mixed_ref, gfin,
     f_ref, pos_ref, shift_ref, gain_ref, off_ref, sharp_ref, wup_ref, wdn_ref, cot_ref,
     zs, arr, arrf, xin, xa, own4, all4, own_sharp, all_sharp, xrow, nall, back, wup_t, wdn_t, low, xt, ctt, mlp, rs, xs, xr, cross,
-    g32, gs16, crecv, db16, drecv, hb16, nr, cb16, fr,
+    g32, gs16, crecv, db16, drecv, hb16, nr, hb2, nr2, cb16, fr,
     zss, zrs, tss, trs, wss, wrs, css, crs, sss, srs, ass, ars, mss, mrs, gss, grs, dss, drs, oss, ors, los,
 ):
     dp = lax.axis_index("dp")
@@ -294,7 +294,7 @@
     steps = (8, 4, 12, 0)
     near_z = (1, -1, 4 * core - 2)
     near_by = (2, -2, 8 * core - 4)
-    cores, twins, near, far = [], [], [], []
+    cores, twins, near, far = [], {}, {}, {}
     for s, k in enumerate(steps):
         for j, d in enumerate((1, -1, 2 - 4 * core, 0)):
             gs16[4 * s + j] = g32[rows_of(1 - core, z + d + k, 0, CHUNK), :].astype(BF16)
@@ -317,14 +317,20 @@
 
     for s, k in enumerate(steps):
         cores[s].wait_recv()
+        if s == 2:
+            for i in range(3):
+                both = g32[rows_of(core, z + near_z[i] + k, 0, CHUNK), :] + crecv[8 + i].astype(F32)
+                hb2[i] = both.astype(BF16)
+                near[6 + i] = remote(hb2.at[i], nr2.at[i], gss.at[6 + i], grs.at[6 + i], table=around(near_by[i]))
+                near[6 + i].start()
+            continue
         for j, d in enumerate(near_z + (0,)):
             n = 4 * s + j
             theirs = g32[rows_of(core, z + d + k, 1 - dp, PIECE), :] + crecv[n, half(1 - dp), :].astype(F32)
             db16[n] = theirs.astype(BF16)
         four = pl.ds(4 * s, 4)
-        copy = remote(db16.at[four], drecv.at[four], dss.at[s], drs.at[s], dp=1 - dp)
-        copy.start()
-        twins.append(copy)
+        twins[s] = remote(db16.at[four], drecv.at[four], dss.at[s], drs.at[s], dp=1 - dp)
+        twins[s].start()
 
     def ours(n, zz):
         total = g32[rows_of(core, zz, dp, PIECE), :] + crecv[n, half(dp), :].astype(F32)
@@ -335,9 +341,8 @@
         for i in range(3):
             n = 3 * s + i
             hb16[n] = ours(4 * s + i, z + near_z[i] + steps[s]).astype(BF16)
-            copy = remote(hb16.at[n], nr.at[n], gss.at[n], grs.at[n], table=around(near_by[i]))
-            copy.start()
-            near.append(copy)
+            near[n] = remote(hb16.at[n], nr.at[n], gss.at[n], grs.at[n], table=around(near_by[i]))
+            near[n].start()
 
     def four_chips(s):
         total = ours(4 * s + 3, z + steps[s])
@@ -346,19 +351,30 @@
             total = total + nr[n].astype(F32)
         return total
 
-    def send_far(s):
-        cb16[s] = four_chips(s).astype(BF16)
-        copy = remote(cb16.at[s], fr.at[s], gss.at[12 + s], grs.at[12 + s], table=around(2 * steps[s]))
-        copy.start()
-        far.append(copy)
+    def far_on(s, total):
+        cb16[s] = total.astype(BF16)
+        far[s] = remote(cb16.at[s], fr.at[s], gss.at[12 + s], grs.at[12 + s], table=around(2 * steps[s]))
+        far[s].start()
 
     send_near(0)
+    for n in range(6, 9):
+        near[n].wait_recv()
+
+    def third(d):
+        total = g32[rows_of(core, z + steps[2], d, PIECE), :] + crecv[11, half(d), :].astype(F32)
+        for i in range(3):
+            total = total + nr2[i, half(d), :].astype(F32)
+        return total
+
+    db16[11] = third(1 - dp).astype(BF16)
+    twins[2] = remote(db16.at[11], drecv.at[11], dss.at[2], drs.at[2], dp=1 - dp)
+    twins[2].start()
     send_near(1)
-    send_far(0)
-    send_near(2)
-    send_far(1)
+    far_on(0, four_chips(0))
+    twins[2].wait_recv()
+    far_on(2, third(dp) + drecv[11].astype(F32))
     send_near(3)
-    send_far(2)
+    far_on(1, four_chips(1))
     for copy in terms:
         copy.wait_recv()
 
@@ -376,8 +392,8 @@
     terms.append(remote(xs, xr, mss.at[6], mrs.at[6], tensor=at(1, 0)))
     terms[6].start()
     total = four_chips(3)
-    for n, copy in enumerate(far):
-        copy.wait_recv()
+    for n in range(3):
+        far[n].wait_recv()
         total = total + fr[n].astype(F32)
     gfin[rows_of(core, z, dp, PIECE), :] = total.astype(BF16)
 
@@ -414,7 +430,7 @@
         back_far[s] = send_same(z, gss, grs, 15 + s, table=around(2 * steps[s]))
     to_near(3)
     to_dp(3, 3)
-    settle(cores, twins, near, far, terms[:6])
+    settle(cores, twins.values(), near.values(), far.values(), terms[:6])
     pass_on(nall.at[tensor], 0, at(1, 0)).wait_send()
     for k in ring:
         pass_on(nall.at[tensor], k, at(0, k)).wait_send()
@@ -548,6 +564,8 @@
         pltpu.VMEM((16, PIECE, 128), BF16),
         pltpu.VMEM((12, PIECE, 128), BF16),
         pltpu.VMEM((12, PIECE, 128), BF16),
+        pltpu.VMEM((3, CHUNK, 128), BF16),
+        pltpu.VMEM((3, CHUNK, 128), BF16),
         pltpu.VMEM((3, PIECE, 128), BF16),
         pltpu.VMEM((3, PIECE, 128), BF16),
     ]

time: 88.9 us -> 87.3 us (0.982)
  Pallas kernels: 87.5 us -> 85.9 us
    pallas_call x1, Pallas kernels: 86 us -> 84.4 us  [body(): pl.pallas_call(kernel, name='layer', out_shape=(pltpu.VMEM((16, 64, 64),...]
where the time goes in v6:
time: 87.3 us; the launch traced here: 87.2 us
  Pallas kernels  85.9 us (98%)
  between operations  1.29 us (1%)
    pallas_call x1, Pallas kernels, body(): pl.pallas_call(kernel, name='layer', out_shape=(pltpu.VMEM((16, 64, 64),...  84.4 us

profile of v6, /device:TPU:1, one launch (start us, length us, event | category | flops | bytes accessed | tf_op | source)
XLA Modules:
  0.0 87.2 jit_solution(2688318161007491313)
XLA Ops:
  1.3 84.4 %layer.1 = (bf16[16,64,64]{2,1,0:T(8,128)(2,1)S(1)}, bf16[5120,128]{1,0:T(8,128)(2,1)S(1)}) custom-call(bf16[128,512]{1,0:T(8,128)(2,1)} %bitcast.15, s32[1,64]{1,0:T(1,128)} %bitcast.18, f32[64,64]{1,0:T(8,128)} %shift_hbm.1, bf16[3,64,512]{2,1,0:T(8,128)(2,1)} %bitcast.14, f32[1,1]{1,0:T(1,128)} %bitcast.12.sharp_hbm, bf16[64,512]{1,0:T(8,128)(2,1)} %mex_hbm.1, ...), custom_call_target="tpu_custom_call" | custom-call | tf_op jit(solution)/shard_map/layer/pallas_call | solution.py:575
  85.6 1.5 %write_out.1 = (bf16[16,64,64]{2,1,0:T(8,128)(2,1)}, f32[64,512]{1,0:T(8,128)}, f32[1,64]{1,0:T(1,128)}, f32[512,512]{1,0:T(8,128)}, f32[512,512]{1,0:T(8,128)}) custom-call(bf16[16,64,64]{2,1,0:T(8,128)(2,1)S(1)} %get-tuple-element.12.mixed_ref, bf16[5120,128]{1,0:T(8,128)(2,1)S(1)} %get-tuple-element.13.g_ref), custom_call_target="tpu_custom_call" | custom-call | tf_op jit(solution)/shard_map/write_out/pallas_call | solution.py:587
